TPU v7x, 256 devices: a whole 4x4x8 slice. The times are simulated.
256 devices in a mesh: prow: 32 (over y, x, core), pcol: 8 (over z).
Axes of the slice: x: 4, y: 4, z: 8, core: 2. Of those that a mesh axis runs over, the one named last changes fastest.
Arguments:
- matrix: bfloat16 [1, 32, 256, 8, 8, 256], P(None, 'prow', None, None, 'pcol'), may hold values from -6 to 6
- linv: bfloat16 [3, 256, 256], replicated, may hold values from -0.25 to 1, as said below
- uinv: bfloat16 [3, 256, 256], replicated, may hold values from -0.002 to 0.0079, as said below
Outputs:
- factored: float32 [1, 32, 256, 8, 8, 256], P(None, 'prow', None, None, 'pcol')
Inputs may be any that keep to these rules, and one draw needn't show every extreme that they name: linv[k] is unit lower triangular. uinv[k] is upper triangular with a positive diagonal.
All inputs are finite; a program needn't handle non-finite values.
Results may differ from a plain program's by a relative error of at most 0.0017.
Values may be sent and summed in bfloat16 or wider, within the bound.
No kernel may reach another device: no remote copies, remote signals or barrier semaphores. Data moves between devices by JAX's collectives and lax.ppermute only.
A program may use at most 64 MiB of HBM per device.

v0:
```python
import jax
import jax.numpy as jnp
from jax import lax
from jax.experimental import pallas as pl
from jax.experimental.pallas import tpu as pltpu
from jax.sharding import PartitionSpec as P

BF = jnp.bfloat16
F32 = jnp.float32


def dev(y, x, c):
    return (y % 4) * 8 + (x % 4) * 2 + c


def mm(a, b):
    return jnp.dot(a, b, preferred_element_type=F32)


def pick(index, options):
    out = options[-1]
    for i in range(len(options) - 2, -1, -1):
        out = jnp.where(index == i, options[i], out)
    return out


class Place:
    def __init__(self, index, count):
        self.index = index
        self.flags = [index == i for i in range(count)]

    def __eq__(self, other):
        return self.flags[other]


def gather_ring(piece, x_core):
    got = {}
    for d in (2, 1, 3):
        pairs = []
        for y in range(4):
            for x in range(4):
                pairs.append((dev(y, x, x_core), dev(y, x + d, x_core)))
                pairs.append((dev(y, x, 1 - x_core), dev(y + d, x, 1 - x_core)))
        got[d] = lax.ppermute(piece, "prow", pairs)
    return [piece, got[1], got[2], got[3]]


def tie(*arrays):
    return lax.optimization_barrier(arrays)


def z_out(b, z):
    up = lax.ppermute(b, "pcol", [(0, 3), (1, 4), (2, 5)])
    down = lax.ppermute(b, "pcol", [(0, 6), (1, 7), (2, 0)])
    return up, down


def z_fill(b, z, up, down):
    own = pick(z, [b, b, b, up, up, up, down, down])
    second = jnp.where(z == 0, down, own)
    above = lax.ppermute(own, "pcol", [(i, (i + 1) % 8) for i in range(8)])
    below = lax.ppermute(second, "pcol", [(i, (i - 1) % 8) for i in range(8)])
    return own, second, above, below


def z_sort(z, own, second, above, below):
    return [
        pick(z, [own, above, below, own, above, below, own, above]),
        pick(z, [below, own, above, below, own, above, below, own]),
        pick(z, [second, below, own, above, below, own, above, below]),
    ]


def solve_kernel(s_ref, mine, other, cmine, cother, linv, uinv, u, small, diag, abuf, cbuf):
    p, z = s_ref[0], s_ref[1]
    x, y, c = (p >> 1) & 3, p >> 3, p & 1

    def assemble(bulk, corner, half):
        for j in range(4):
            for i in range(4):
                if half == 0:
                    g = 4 * ((y - j) & 3) + ((x - i) & 3)
                else:
                    g = 4 * ((y - i) & 3) + ((x - j) & 3)
                rows = pl.ds(pl.multiple_of(16 * g, 16), 16)
                for r in range(3):
                    at = 192 * j + 48 * i + 16 * r
                    part = bulk[at : at + 16, :]
                    abuf[r, rows, 128 * half : 128 * half + 128] = part[:, 0:128]
                    lane = 256 + 896 * half
                    abuf[r, rows, lane : lane + 896] = part[:, 128:1024]
                    for q in range(2):
                        at = 384 * j + 128 * r + 64 * q + 16 * i
                        cbuf[r, q, rows, 128 * half : 128 * half + 128] = corner[at : at + 16, :]

    @pl.when(c == 0)
    def _():
        assemble(mine, cmine, 0)
        assemble(other, cother, 1)

    @pl.when(c == 1)
    def _():
        assemble(other, cother, 0)
        assemble(mine, cmine, 1)

    a10, a20 = cbuf[0, 0], cbuf[0, 1]
    a01, a21 = cbuf[1, 0], cbuf[1, 1]
    a02, a12 = cbuf[2, 0], cbuf[2, 1]
    u01 = mm(linv[0], a01).astype(BF)
    u02 = mm(linv[0], a02).astype(BF)
    l10 = mm(a10, uinv[0]).astype(BF)
    l20 = mm(a20, uinv[0]).astype(BF)
    u12 = mm(linv[1], (a12.astype(F32) - mm(l10, u02)).astype(BF)).astype(BF)
    l21 = mm((a21.astype(F32) - mm(l20, u01)).astype(BF), uinv[1]).astype(BF)
    small[0], small[1], small[2] = u01, u02, u12
    u0 = mm(linv[0], abuf[0]).astype(BF)
    u[0:256, :] = u0
    s1 = abuf[1].astype(F32) - mm(l10, u0)
    u1 = mm(linv[1], s1.astype(BF)).astype(BF)
    u[256:512, :] = u1
    s2 = abuf[2].astype(F32) - mm(l20, u0) - mm(l21, u1)
    u[512:768, :] = mm(linv[2], s2.astype(BF)).astype(BF)
    diag[...] = jnp.where(z == 1, s1[:, :256], s2[:, :256])


def solve(*operands):
    return pl.pallas_call(
        solve_kernel,
        out_shape=[
            jax.ShapeDtypeStruct((768, 2048), BF),
            jax.ShapeDtypeStruct((3, 256, 256), BF),
            jax.ShapeDtypeStruct((256, 256), F32),
        ],
        in_specs=[pl.BlockSpec(memory_space=pltpu.SMEM)]
        + [pl.BlockSpec(memory_space=pltpu.VMEM)] * 6,
        out_specs=[pl.BlockSpec(memory_space=pltpu.VMEM)] * 3,
        scratch_shapes=[pltpu.VMEM((3, 256, 2048), BF), pltpu.VMEM((3, 2, 256, 256), BF)],
        compiler_params=pltpu.CompilerParams(vmem_limit_bytes=24 * 1024 * 1024),
        cost_estimate=pl.CostEstimate(
            flops=1_700_000_000, bytes_accessed=10_000_000, transcendentals=0
        ),
    )(*operands)


def finish_kernel(s_ref, u, small, diag, w, own, own5, above, below, uinv, out, lbuf):
    p, z = s_ref[0], s_ref[1]
    b0, b1, b2 = z_sort(z, own[...], own5[...], above[...], below[...])
    u01, u02, u12 = small[0], small[1], small[2]
    l0 = mm(b0, uinv[0]).astype(BF)
    l1 = mm((b1.astype(F32) - mm(l0, u01)).astype(BF), uinv[1]).astype(BF)
    l2 = mm((b2.astype(F32) - mm(l0, u02) - mm(l1, u12)).astype(BF), uinv[2]).astype(BF)
    rows = lax.broadcasted_iota(jnp.int32, (256, 256), 0)
    cols = lax.broadcasted_iota(jnp.int32, (256, 256), 1)
    minus_one = jnp.where(rows == cols, -1.0, 0.0).astype(BF)
    zero = jnp.zeros((256, 256), BF)
    lbuf[:, 0:256] = pick(p, [minus_one, zero, zero, l0])
    lbuf[:, 256:512] = pick(p, [zero, minus_one, zero, l1])
    lbuf[:, 512:768] = pick(p, [zero, zero, minus_one, l2])
    keep = jnp.where(p < 3, 0.0, 1.0)
    res = w[...].astype(F32) * keep - mm(lbuf[...], u[...])
    for k in range(16):
        out[pl.ds(k, 256, stride=16), :] = res[:, 128 * k : 128 * k + 128]

    @pl.when(z < 3)
    def _():
        panel = pick(z, [l0.astype(F32), l1.astype(F32), l2.astype(F32)])
        middle = jnp.where(z == 0, w[:, :256].astype(F32), diag[...])
        special = jnp.where(p > z, panel, jnp.where(p == z, middle, res[:, :256]))
        out[pl.ds(0, 256, stride=16), :] = special[:, :128]
        out[pl.ds(1, 256, stride=16), :] = special[:, 128:]


def finish(*operands):
    return pl.pallas_call(
        finish_kernel,
        out_shape=jax.ShapeDtypeStruct((4096, 128), F32),
        in_specs=[pl.BlockSpec(memory_space=pltpu.SMEM)]
        + [pl.BlockSpec(memory_space=pltpu.VMEM)] * 9,
        out_specs=pl.BlockSpec(memory_space=pltpu.VMEM),
        scratch_shapes=[pltpu.VMEM((256, 768), BF)],
        compiler_params=pltpu.CompilerParams(vmem_limit_bytes=24 * 1024 * 1024),
        cost_estimate=pl.CostEstimate(
            flops=900_000_000, bytes_accessed=7_000_000, transcendentals=0
        ),
    )(*operands)


def swap_cores(a):
    return lax.ppermute(a, "prow", [(i, i ^ 1) for i in range(32)])


def body(matrix, linv, uinv):
    p, z = lax.axis_index("prow"), lax.axis_index("pcol")
    scalars = jnp.stack([p, z]).astype(jnp.int32)
    z = Place(z, 8)
    matrix, scalars, *z.flags = tie(matrix, scalars, *z.flags)
    w = matrix.reshape(256, 2048)
    panel = w[:, :256]
    up, down = z_out(panel, z)
    halves = jnp.stack(
        [
            jnp.concatenate([w[:, :128], w[:, 256:1152]], axis=1),
            jnp.concatenate([w[:, 128:256], w[:, 1152:]], axis=1),
        ]
    )
    parts = halves.reshape(2, 16, 16, 1024).transpose(1, 0, 2, 3).reshape(32, 16, 1024)
    piece = lax.all_to_all(parts, "prow", 0, 0)[:3].reshape(48, 1024)
    piece, up, down = tie(piece, up, down)
    line = jnp.concatenate(gather_ring(piece, 0))
    blocks = [
        jnp.concatenate([line[48 * i + 16 * r : 48 * i + 16 * r + 16, :128] for i in range(4)])
        for r in range(3)
    ]
    edge = jnp.concatenate(
        [
            jnp.where(z == 0, blocks[1], blocks[0]),
            jnp.where(z == 2, blocks[1], blocks[2]),
        ]
    )
    edge_out = z_out(edge, z)
    mine = gather_ring(line, 1)
    *mine, edge_up, edge_down = tie(*mine, *edge_out)
    mine = jnp.concatenate(mine)
    other = swap_cores(mine)
    corner = jnp.concatenate(z_sort(z, *z_fill(edge, z, edge_up, edge_down)))
    cmine = gather_ring(corner, 1)
    cmine[2], up, down = tie(cmine[2], up, down)
    filled = z_fill(panel, z, up, down)
    cother = swap_cores(jnp.concatenate(cmine))
    cmine = jnp.concatenate(cmine)
    u, small, diag = solve(scalars, mine, other, cmine, cother, linv, uinv)
    out = finish(scalars, u, small, diag, w, *filled, uinv)
    return out.reshape(matrix.shape)


def solution(mesh):
    in_specs = (P(None, "prow", None, None, "pcol", None), P(), P())
    out_specs = P(None, "prow", None, None, "pcol", None)
    return jax.shard_map(body, mesh=mesh, in_specs=in_specs, out_specs=out_specs, check_vma=False)
```

profile of v0, /device:TPU:1, one launch (start us, length us, event | category | flops | bytes accessed | tf_op | source)
XLA Modules:
  0.0 79.3 jit_solution(10920031670664459140)
XLA Ops:
  0.1 1.5 %copy.8 = bf16[32,8,8,256]{3,1,2,0:T(8,128)(2,1)S(1)} copy(bf16[32,8,8,256]{3,2,1,0:T(8,128)(2,1)} %bitcast.24) | data formatting | bytes 2097152
  1.7 0.1 pad_maximum_fusion.1
  1.9 1.1 %pad_maximum_fusion = bf16[2,16,16,1024]{3,2,0,1:T(8,128)(2,1)} fusion(bf16[1,16,16,1024]{3,2,0,1:T(8,128)(2,1)S(1)} %bitcast.23, bf16[1,16,16,1024]{3,2,0,1:T(8,128)(2,1)S(1)} %bitcast.22), kind=kLoop, calls=%fused_computation | loop fusion | flops 524288 | bytes 2097152 | tf_op jit(solution)/shard_map/stack | solution.py:200
  2.9 8.6 %all-to-all-start = ((bf16[32,16,1024]{2,1,0:T(8,128)(2,1)}), bf16[32,16,1024]{2,1,0:T(8,128)(2,1)S(1)}, u32[]{:S(2)}, u32[]{:S(2)}) async-start(bf16[32,16,1024]{2,1,0:T(8,128)(2,1)} %bitcast.7), calls=%async_computation | async-start | bytes 2097152 | tf_op jit(solution)/shard_map/all_to_all | solution.py:207
  11.6 6.3 %collective-permute-start = (bf16[256,256]{1,0:T(8,128)(2,1)S(1)}, bf16[256,256]{1,0:T(8,128)(2,1)S(1)}, u32[]{:S(2)}, u32[]{:S(2)}) collective-permute-start(bf16[256,256]{1,0:T(8,128)(2,1)S(1)} %slice.77), channel_id=1, source_target_pairs={{0,3},{1,4},{2,5},{8,11},{9,12},{10,13},{16,19},{17,20},{18,21},{2... | collective-permute-start | bytes 393224 | tf_op jit(solution)/shard_map/ppermute | solution.py:53
  17.8 2.3 %collective-permute-start.1 = (bf16[256,256]{1,0:T(8,128)(2,1)S(1)}, bf16[256,256]{1,0:T(8,128)(2,1)S(1)}, u32[]{:S(2)}, u32[]{:S(2)}) collective-permute-start(bf16[256,256]{1,0:T(8,128)(2,1)S(1)} %slice.77), channel_id=1, source_target_pairs={{0,6},{1,7},{2,0},{8,14},{9,15},{10,8},{16,22},{17,23},{18,16},{24... | collective-permute-start | bytes 393224 | tf_op jit(solution)/shard_map/ppermute | solution.py:54
  20.2 8.5 %all-to-all-done = bf16[32,16,1024]{2,1,0:T(8,128)(2,1)S(1)} async-done(((bf16[32,16,1024]{2,1,0:T(8,128)(2,1)}), bf16[32,16,1024]{2,1,0:T(8,128)(2,1)S(1)}, u32[]{:S(2)}, u32[]{:S(2)}) %all-to-all-start) | async-done | bytes 1048608 | tf_op jit(solution)/shard_map/all_to_all | solution.py:207
  28.7 0.1 collective-permute-start.2
  28.8 1.7 %collective-permute-start.3 = (bf16[48,1024]{1,0:T(8,128)(2,1)S(1)}, bf16[48,1024]{1,0:T(8,128)(2,1)S(1)}, u32[]{:S(2)}, u32[]{:S(2)}) collective-permute-start(bf16[48,1024]{1,0:T(8,128)(2,1)S(1)} %bitcast.26), channel_id=1, source_target_pairs={{0,32},{8,136},{16,48},{24,152},{32,0},{40,168},{48,16},{56,184},{... | collective-permute-start | bytes 294920 | tf_op jit(solution)/shard_map/ppermute | solution.py:44
  30.5 1.4 %collective-permute-start.4 = (bf16[48,1024]{1,0:T(8,128)(2,1)S(1)}, bf16[48,1024]{1,0:T(8,128)(2,1)S(1)}, u32[]{:S(2)}, u32[]{:S(2)}) collective-permute-start(bf16[48,1024]{1,0:T(8,128)(2,1)S(1)} %bitcast.27), channel_id=1, source_target_pairs={{0,48},{8,200},{16,0},{24,216},{32,16},{40,232},{48,32},{56,248},{... | collective-permute-start | bytes 294920 | tf_op jit(solution)/shard_map/ppermute | solution.py:44
  31.9 2.9 %collective-permute-done.2 = bf16[48,1024]{1,0:T(8,128)(2,1)S(1)} collective-permute-done((bf16[48,1024]{1,0:T(8,128)(2,1)S(1)}, bf16[48,1024]{1,0:T(8,128)(2,1)S(1)}, u32[]{:S(2)}, u32[]{:S(2)}) %collective-permute-start.2) | collective-permute-done | bytes 98336 | tf_op jit(solution)/shard_map/ppermute | solution.py:44
  34.9 0.5 collective-permute-done.4
  35.4 0.4 collective-permute-start.5
  35.9 1.8 %collective-permute-start.6 = (bf16[192,1024]{1,0:T(8,128)(2,1)S(1)}, bf16[192,1024]{1,0:T(8,128)(2,1)S(1)}, u32[]{:S(2)}, u32[]{:S(2)}) collective-permute-start(bf16[192,1024]{1,0:T(8,128)(2,1)S(1)} %constant_dynamic-update-slice_fusion), channel_id=1, source_target_pairs={{8,40},{0,128},{24,56},{16,144},{40,8},{32,160},{56,24},{48,176},{... | collective-permute-start | bytes 1179656 | tf_op jit(solution)/shard_map/ppermute | solution.py:44
  37.7 0.8 %collective-permute-start.7 = (bf16[192,1024]{1,0:T(8,128)(2,1)S(1)}, bf16[192,1024]{1,0:T(8,128)(2,1)S(1)}, u32[]{:S(2)}, u32[]{:S(2)}) collective-permute-start(bf16[192,1024]{1,0:T(8,128)(2,1)S(1)} %constant_dynamic-update-slice_fusion), channel_id=1, source_target_pairs={{8,56},{0,192},{24,8},{16,208},{40,24},{32,224},{56,40},{48,240},{... | collective-permute-start | bytes 1179656 | tf_op jit(solution)/shard_map/ppermute | solution.py:44
  38.6 6.3 %collective-permute-start.8 = (bf16[128,128]{1,0:T(8,128)(2,1)S(1)}, bf16[128,128]{1,0:T(8,128)(2,1)S(1)}, u32[]{:S(2)}, u32[]{:S(2)}) collective-permute-start(bf16[128,128]{1,0:T(8,128)(2,1)S(1)} %pad_maximum_fusion.4), channel_id=1, source_target_pairs={{0,3},{1,4},{2,5},{8,11},{9,12},{10,13},{16,19},{17,20},{18,21},{2... | collective-permute-start | bytes 98312 | tf_op jit(solution)/shard_map/ppermute | solution.py:53
  44.9 2.3 %collective-permute-start.9 = (bf16[128,128]{1,0:T(8,128)(2,1)S(1)}, bf16[128,128]{1,0:T(8,128)(2,1)S(1)}, u32[]{:S(2)}, u32[]{:S(2)}) collective-permute-start(bf16[128,128]{1,0:T(8,128)(2,1)S(1)} %pad_maximum_fusion.4), channel_id=1, source_target_pairs={{0,6},{1,7},{2,0},{8,14},{9,15},{10,8},{16,22},{17,23},{18,16},{24... | collective-permute-start | bytes 98312 | tf_op jit(solution)/shard_map/ppermute | solution.py:54
  47.2 3.7 %collective-permute-done.9 = bf16[128,128]{1,0:T(8,128)(2,1)S(1)} collective-permute-done((bf16[128,128]{1,0:T(8,128)(2,1)S(1)}, bf16[128,128]{1,0:T(8,128)(2,1)S(1)}, u32[]{:S(2)}, u32[]{:S(2)}) %collective-permute-start.9) | collective-permute-done | bytes 32800 | tf_op jit(solution)/shard_map/ppermute | solution.py:54
  51.1 0.1 collective-permute-start.11
  51.1 3.1 %collective-permute-start.12 = (bf16[128,128]{1,0:T(8,128)(2,1)S(1)}, bf16[128,128]{1,0:T(8,128)(2,1)S(1)}, u32[]{:S(2)}, u32[]{:S(2)}) collective-permute-start(bf16[128,128]{1,0:T(8,128)(2,1)S(1)} %get-tuple-element.61), channel_id=1, source_target_pairs={{0,7},{1,0},{2,1},{3,2},{4,3},{5,4},{6,5},{7,6},{8,15},{9,8},{10,9... | collective-permute-start | bytes 98312 | tf_op jit(solution)/shard_map/ppermute | solution.py:62
  54.4 4.1 %collective-permute-start.10 = (bf16[768,1024]{1,0:T(8,128)(2,1)S(1)}, bf16[768,1024]{1,0:T(8,128)(2,1)S(1)}, u32[]{:S(2)}, u32[]{:S(2)}) collective-permute-start(bf16[768,1024]{1,0:T(8,128)(2,1)S(1)} %constant_dynamic-update-slice_fusion.4.mine), channel_id=1, source_target_pairs={{0,8},{8,0},{16,24},{24,16},{32,40},{40,32},{48,56},{56,48},{64,72... | collective-permute-start | bytes 4718600 | tf_op jit(solution)/shard_map/ppermute | solution.py:189
  58.7 1.9 %collective-permute-start.14 = (bf16[384,128]{1,0:T(8,128)(2,1)S(1)}, bf16[384,128]{1,0:T(8,128)(2,1)S(1)}, u32[]{:S(2)}, u32[]{:S(2)}) collective-permute-start(bf16[384,128]{1,0:T(8,128)(2,1)S(1)} %pad_maximum_fusion.3), channel_id=1, source_target_pairs={{8,40},{0,128},{24,56},{16,144},{40,8},{32,160},{56,24},{48,176},{... | collective-permute-start | bytes 294920 | tf_op jit(solution)/shard_map/ppermute | solution.py:44
  60.5 1.1 %collective-permute-start.13 = (bf16[384,128]{1,0:T(8,128)(2,1)S(1)}, bf16[384,128]{1,0:T(8,128)(2,1)S(1)}, u32[]{:S(2)}, u32[]{:S(2)}) collective-permute-start(bf16[384,128]{1,0:T(8,128)(2,1)S(1)} %pad_maximum_fusion.3), channel_id=1, source_target_pairs={{8,24},{0,64},{24,40},{16,80},{40,56},{32,96},{56,8},{48,112},{72,... | collective-permute-start | bytes 294920 | tf_op jit(solution)/shard_map/ppermute | solution.py:44
  61.6 1.6 %collective-permute-start.15 = (bf16[384,128]{1,0:T(8,128)(2,1)S(1)}, bf16[384,128]{1,0:T(8,128)(2,1)S(1)}, u32[]{:S(2)}, u32[]{:S(2)}) collective-permute-start(bf16[384,128]{1,0:T(8,128)(2,1)S(1)} %pad_maximum_fusion.3), channel_id=1, source_target_pairs={{8,56},{0,192},{24,8},{16,208},{40,24},{32,224},{56,40},{48,240},{... | collective-permute-start | bytes 294920 | tf_op jit(solution)/shard_map/ppermute | solution.py:44
  63.2 0.5 collective-permute-done.14
  63.7 1.8 %collective-permute-done.13 = bf16[384,128]{1,0:T(8,128)(2,1)S(1)} collective-permute-done((bf16[384,128]{1,0:T(8,128)(2,1)S(1)}, bf16[384,128]{1,0:T(8,128)(2,1)S(1)}, u32[]{:S(2)}, u32[]{:S(2)}) %collective-permute-start.13) | collective-permute-done | bytes 98336 | tf_op jit(solution)/shard_map/ppermute | solution.py:44
  65.6 2.9 %collective-permute-start.16 = (bf16[1536,128]{1,0:T(8,128)(2,1)S(1)}, bf16[1536,128]{1,0:T(8,128)(2,1)S(1)}, u32[]{:S(2)}, u32[]{:S(2)}) collective-permute-start(bf16[1536,128]{1,0:T(8,128)(2,1)S(1)} %constant_dynamic-update-slice_fusion.8.cmine), channel_id=1, source_target_pairs={{0,8},{8,0},{16,24},{24,16},{32,40},{40,32},{48,56},{56,48},{64,72... | collective-permute-start | bytes 1179656 | tf_op jit(solution)/shard_map/ppermute | solution.py:189
  68.5 0.1 collective-permute-start.17
  68.6 3.2 %collective-permute-start.18 = (bf16[256,256]{1,0:T(8,128)(2,1)S(1)}, bf16[256,256]{1,0:T(8,128)(2,1)S(1)}, u32[]{:S(2)}, u32[]{:S(2)}) collective-permute-start(bf16[256,256]{1,0:T(8,128)(2,1)S(1)} %get-tuple-element.53.own5), channel_id=1, source_target_pairs={{0,7},{1,0},{2,1},{3,2},{4,3},{5,4},{6,5},{7,6},{8,15},{9,8},{10,9... | collective-permute-start | bytes 393224 | tf_op jit(solution)/shard_map/ppermute | solution.py:62
  71.9 3.3 %shard_map.37 = (bf16[768,2048]{1,0:T(8,128)(2,1)S(1)}, bf16[3,256,256]{2,1,0:T(8,128)(2,1)S(1)}, f32[256,256]{1,0:T(8,128)S(1)}) custom-call(s32[2]{0:T(128)S(1)} %pad_add_fusion.s_ref, bf16[768,1024]{1,0:T(8,128)(2,1)S(1)} %constant_dynamic-update-slice_fusion.4.mine, bf16[768,1024]{1,0:T(8,128)(2,1)S(1)} %collective-permute-done.10.other, ...), custom_call_target="tpu_custom_call" | custom-call | flops 1700000000 | bytes 10000000 | tf_op jit(solution)/shard_map/pallas_call | solution.py:127
  75.2 0.2 collective-permute-done.17.above
  75.4 3.9 %shard_map.38 = f32[4096,128]{1,0:T(8,128)} custom-call(s32[2]{0:T(128)S(1)} %pad_add_fusion.s_ref, bf16[768,2048]{1,0:T(8,128)(2,1)S(1)} %get-tuple-element.48.u, bf16[3,256,256]{2,1,0:T(8,128)(2,1)S(1)} %get-tuple-element.49.small, f32[256,256]{1,0:T(8,128)S(1)} %get-tuple-element.50.diag, bf16[256,2048]{1,0:T(8,128)(2,1)S(1)} %bitcast.21, ...), custom_call_target="tpu_custom_call" | custom-call | flops 900000000 | bytes 7000000 | tf_op jit(solution)/shard_map/pallas_call | solution.py:174
  (45 shorter events, 0.7 us)
Async XLA Ops:
  2.9 25.8 %all-to-all-start = ((bf16[32,16,1024]{2,1,0:T(8,128)(2,1)}), bf16[32,16,1024]{2,1,0:T(8,128)(2,1)S(1)}, u32[]{:S(2)}, u32[]{:S(2)}) async-start(bf16[32,16,1024]{2,1,0:T(8,128)(2,1)} %bitcast.7), calls=%async_computation | async-start | bytes 2097152 | tf_op jit(solution)/shard_map/all_to_all | solution.py:207
  11.6 17.2 %collective-permute-start = (bf16[256,256]{1,0:T(8,128)(2,1)S(1)}, bf16[256,256]{1,0:T(8,128)(2,1)S(1)}, u32[]{:S(2)}, u32[]{:S(2)}) collective-permute-start(bf16[256,256]{1,0:T(8,128)(2,1)S(1)} %slice.77), channel_id=1, source_target_pairs={{0,3},{1,4},{2,5},{8,11},{9,12},{10,13},{16,19},{17,20},{18,21},{2... | collective-permute-start | bytes 393224 | tf_op jit(solution)/shard_map/ppermute | solution.py:53
  17.8 10.9 %collective-permute-start.1 = (bf16[256,256]{1,0:T(8,128)(2,1)S(1)}, bf16[256,256]{1,0:T(8,128)(2,1)S(1)}, u32[]{:S(2)}, u32[]{:S(2)}) collective-permute-start(bf16[256,256]{1,0:T(8,128)(2,1)S(1)} %slice.77), channel_id=1, source_target_pairs={{0,6},{1,7},{2,0},{8,14},{9,15},{10,8},{16,22},{17,23},{18,16},{24... | collective-permute-start | bytes 393224 | tf_op jit(solution)/shard_map/ppermute | solution.py:54
  28.7 6.1 %collective-permute-start.2 = (bf16[48,1024]{1,0:T(8,128)(2,1)S(1)}, bf16[48,1024]{1,0:T(8,128)(2,1)S(1)}, u32[]{:S(2)}, u32[]{:S(2)}) collective-permute-start(bf16[48,1024]{1,0:T(8,128)(2,1)S(1)} %bitcast.25), channel_id=1, source_target_pairs={{0,16},{8,72},{16,32},{24,88},{32,48},{40,104},{48,0},{56,120},{64... | collective-permute-start | bytes 294920 | tf_op jit(solution)/shard_map/ppermute | solution.py:44
  28.8 6.0 %collective-permute-start.3 = (bf16[48,1024]{1,0:T(8,128)(2,1)S(1)}, bf16[48,1024]{1,0:T(8,128)(2,1)S(1)}, u32[]{:S(2)}, u32[]{:S(2)}) collective-permute-start(bf16[48,1024]{1,0:T(8,128)(2,1)S(1)} %bitcast.26), channel_id=1, source_target_pairs={{0,32},{8,136},{16,48},{24,152},{32,0},{40,168},{48,16},{56,184},{... | collective-permute-start | bytes 294920 | tf_op jit(solution)/shard_map/ppermute | solution.py:44
  30.5 4.9 %collective-permute-start.4 = (bf16[48,1024]{1,0:T(8,128)(2,1)S(1)}, bf16[48,1024]{1,0:T(8,128)(2,1)S(1)}, u32[]{:S(2)}, u32[]{:S(2)}) collective-permute-start(bf16[48,1024]{1,0:T(8,128)(2,1)S(1)} %bitcast.27), channel_id=1, source_target_pairs={{0,48},{8,200},{16,0},{24,216},{32,16},{40,232},{48,32},{56,248},{... | collective-permute-start | bytes 294920 | tf_op jit(solution)/shard_map/ppermute | solution.py:44
  35.4 15.5 %collective-permute-start.5 = (bf16[192,1024]{1,0:T(8,128)(2,1)S(1)}, bf16[192,1024]{1,0:T(8,128)(2,1)S(1)}, u32[]{:S(2)}, u32[]{:S(2)}) collective-permute-start(bf16[192,1024]{1,0:T(8,128)(2,1)S(1)} %constant_dynamic-update-slice_fusion), channel_id=1, source_target_pairs={{8,24},{0,64},{24,40},{16,80},{40,56},{32,96},{56,8},{48,112},{72,... | collective-permute-start | bytes 1179656 | tf_op jit(solution)/shard_map/ppermute | solution.py:44
  35.9 15.1 %collective-permute-start.6 = (bf16[192,1024]{1,0:T(8,128)(2,1)S(1)}, bf16[192,1024]{1,0:T(8,128)(2,1)S(1)}, u32[]{:S(2)}, u32[]{:S(2)}) collective-permute-start(bf16[192,1024]{1,0:T(8,128)(2,1)S(1)} %constant_dynamic-update-slice_fusion), channel_id=1, source_target_pairs={{8,40},{0,128},{24,56},{16,144},{40,8},{32,160},{56,24},{48,176},{... | collective-permute-start | bytes 1179656 | tf_op jit(solution)/shard_map/ppermute | solution.py:44
  37.7 13.3 %collective-permute-start.7 = (bf16[192,1024]{1,0:T(8,128)(2,1)S(1)}, bf16[192,1024]{1,0:T(8,128)(2,1)S(1)}, u32[]{:S(2)}, u32[]{:S(2)}) collective-permute-start(bf16[192,1024]{1,0:T(8,128)(2,1)S(1)} %constant_dynamic-update-slice_fusion), channel_id=1, source_target_pairs={{8,56},{0,192},{24,8},{16,208},{40,24},{32,224},{56,40},{48,240},{... | collective-permute-start | bytes 1179656 | tf_op jit(solution)/shard_map/ppermute | solution.py:44
  38.6 8.7 %collective-permute-start.8 = (bf16[128,128]{1,0:T(8,128)(2,1)S(1)}, bf16[128,128]{1,0:T(8,128)(2,1)S(1)}, u32[]{:S(2)}, u32[]{:S(2)}) collective-permute-start(bf16[128,128]{1,0:T(8,128)(2,1)S(1)} %pad_maximum_fusion.4), channel_id=1, source_target_pairs={{0,3},{1,4},{2,5},{8,11},{9,12},{10,13},{16,19},{17,20},{18,21},{2... | collective-permute-start | bytes 98312 | tf_op jit(solution)/shard_map/ppermute | solution.py:53
  44.9 6.1 %collective-permute-start.9 = (bf16[128,128]{1,0:T(8,128)(2,1)S(1)}, bf16[128,128]{1,0:T(8,128)(2,1)S(1)}, u32[]{:S(2)}, u32[]{:S(2)}) collective-permute-start(bf16[128,128]{1,0:T(8,128)(2,1)S(1)} %pad_maximum_fusion.4), channel_id=1, source_target_pairs={{0,6},{1,7},{2,0},{8,14},{9,15},{10,8},{16,22},{17,23},{18,16},{24... | collective-permute-start | bytes 98312 | tf_op jit(solution)/shard_map/ppermute | solution.py:54
  51.1 7.5 %collective-permute-start.11 = (bf16[128,128]{1,0:T(8,128)(2,1)S(1)}, bf16[128,128]{1,0:T(8,128)(2,1)S(1)}, u32[]{:S(2)}, u32[]{:S(2)}) collective-permute-start(bf16[128,128]{1,0:T(8,128)(2,1)S(1)} %get-tuple-element.62), channel_id=1, source_target_pairs={{0,1},{1,2},{2,3},{3,4},{4,5},{5,6},{6,7},{7,0},{8,9},{9,10},{10,1... | collective-permute-start | bytes 98312 | tf_op jit(solution)/shard_map/ppermute | solution.py:61
  51.1 7.4 %collective-permute-start.12 = (bf16[128,128]{1,0:T(8,128)(2,1)S(1)}, bf16[128,128]{1,0:T(8,128)(2,1)S(1)}, u32[]{:S(2)}, u32[]{:S(2)}) collective-permute-start(bf16[128,128]{1,0:T(8,128)(2,1)S(1)} %get-tuple-element.61), channel_id=1, source_target_pairs={{0,7},{1,0},{2,1},{3,2},{4,3},{5,4},{6,5},{7,6},{8,15},{9,8},{10,9... | collective-permute-start | bytes 98312 | tf_op jit(solution)/shard_map/ppermute | solution.py:62
  54.3 17.5 %copy-start = (bf16[3,256,256]{2,1,0:T(8,128)(2,1)S(1)}, bf16[3,256,256]{2,1,0:T(8,128)(2,1)}, u32[]{:S(2)}) copy-start(bf16[3,256,256]{2,1,0:T(8,128)(2,1)} %uinv.3) | copy-start | bytes 1179652
  54.4 17.5 %copy-start.1 = (bf16[3,256,256]{2,1,0:T(8,128)(2,1)S(1)}, bf16[3,256,256]{2,1,0:T(8,128)(2,1)}, u32[]{:S(2)}) copy-start(bf16[3,256,256]{2,1,0:T(8,128)(2,1)} %linv.1) | copy-start | bytes 1179652
  54.4 17.4 %collective-permute-start.10 = (bf16[768,1024]{1,0:T(8,128)(2,1)S(1)}, bf16[768,1024]{1,0:T(8,128)(2,1)S(1)}, u32[]{:S(2)}, u32[]{:S(2)}) collective-permute-start(bf16[768,1024]{1,0:T(8,128)(2,1)S(1)} %constant_dynamic-update-slice_fusion.4.mine), channel_id=1, source_target_pairs={{0,8},{8,0},{16,24},{24,16},{32,40},{40,32},{48,56},{56,48},{64,72... | collective-permute-start | bytes 4718600 | tf_op jit(solution)/shard_map/ppermute | solution.py:189
  58.7 5.1 %collective-permute-start.14 = (bf16[384,128]{1,0:T(8,128)(2,1)S(1)}, bf16[384,128]{1,0:T(8,128)(2,1)S(1)}, u32[]{:S(2)}, u32[]{:S(2)}) collective-permute-start(bf16[384,128]{1,0:T(8,128)(2,1)S(1)} %pad_maximum_fusion.3), channel_id=1, source_target_pairs={{8,40},{0,128},{24,56},{16,144},{40,8},{32,160},{56,24},{48,176},{... | collective-permute-start | bytes 294920 | tf_op jit(solution)/shard_map/ppermute | solution.py:44
  60.5 5.0 %collective-permute-start.13 = (bf16[384,128]{1,0:T(8,128)(2,1)S(1)}, bf16[384,128]{1,0:T(8,128)(2,1)S(1)}, u32[]{:S(2)}, u32[]{:S(2)}) collective-permute-start(bf16[384,128]{1,0:T(8,128)(2,1)S(1)} %pad_maximum_fusion.3), channel_id=1, source_target_pairs={{8,24},{0,64},{24,40},{16,80},{40,56},{32,96},{56,8},{48,112},{72,... | collective-permute-start | bytes 294920 | tf_op jit(solution)/shard_map/ppermute | solution.py:44
  61.6 3.9 %collective-permute-start.15 = (bf16[384,128]{1,0:T(8,128)(2,1)S(1)}, bf16[384,128]{1,0:T(8,128)(2,1)S(1)}, u32[]{:S(2)}, u32[]{:S(2)}) collective-permute-start(bf16[384,128]{1,0:T(8,128)(2,1)S(1)} %pad_maximum_fusion.3), channel_id=1, source_target_pairs={{8,56},{0,192},{24,8},{16,208},{40,24},{32,224},{56,40},{48,240},{... | collective-permute-start | bytes 294920 | tf_op jit(solution)/shard_map/ppermute | solution.py:44
  65.6 6.3 %collective-permute-start.16 = (bf16[1536,128]{1,0:T(8,128)(2,1)S(1)}, bf16[1536,128]{1,0:T(8,128)(2,1)S(1)}, u32[]{:S(2)}, u32[]{:S(2)}) collective-permute-start(bf16[1536,128]{1,0:T(8,128)(2,1)S(1)} %constant_dynamic-update-slice_fusion.8.cmine), channel_id=1, source_target_pairs={{0,8},{8,0},{16,24},{24,16},{32,40},{40,32},{48,56},{56,48},{64,72... | collective-permute-start | bytes 1179656 | tf_op jit(solution)/shard_map/ppermute | solution.py:189
  68.5 6.9 %collective-permute-start.17 = (bf16[256,256]{1,0:T(8,128)(2,1)S(1)}, bf16[256,256]{1,0:T(8,128)(2,1)S(1)}, u32[]{:S(2)}, u32[]{:S(2)}) collective-permute-start(bf16[256,256]{1,0:T(8,128)(2,1)S(1)} %get-tuple-element.54.own), channel_id=1, source_target_pairs={{0,1},{1,2},{2,3},{3,4},{4,5},{5,6},{6,7},{7,0},{8,9},{9,10},{10,1... | collective-permute-start | bytes 393224 | tf_op jit(solution)/shard_map/ppermute | solution.py:61
  68.6 6.8 %collective-permute-start.18 = (bf16[256,256]{1,0:T(8,128)(2,1)S(1)}, bf16[256,256]{1,0:T(8,128)(2,1)S(1)}, u32[]{:S(2)}, u32[]{:S(2)}) collective-permute-start(bf16[256,256]{1,0:T(8,128)(2,1)S(1)} %get-tuple-element.53.own5), channel_id=1, source_target_pairs={{0,7},{1,0},{2,1},{3,2},{4,3},{5,4},{6,5},{7,6},{8,15},{9,8},{10,9... | collective-permute-start | bytes 393224 | tf_op jit(solution)/shard_map/ppermute | solution.py:62
where the time goes:
time: 79.6 us; the launch traced here: 79.3 us
  starting transfers between devices  50.1 us (63%)
  waiting for transfers between devices  18.3 us (23%)
  Pallas kernels  7.21 us (9%)
  local copies, waits for them, and re-layouts  1.86 us (2%)
  other arithmetic  1.51 us (2%)
    ppermute x2, starting transfers between devices, z_out(): up = lax.ppermute(b, 'pcol', [(0, 3), (1, 4), (2, 5)])  12.6 us
    ppermute x9, starting transfers between devices, gather_ring(): got[d] = lax.ppermute(piece, 'prow', pairs)  10.8 us
    all_to_all x1, starting transfers between devices, body(): piece = lax.all_to_all(parts, 'prow', 0, 0)[:3].reshape(48, 1024)  8.59 us
    all_to_all x1, waiting for transfers between devices, body(): piece = lax.all_to_all(parts, 'prow', 0, 0)[:3].reshape(48, 1024)  8.53 us
    ppermute x2, starting transfers between devices, swap_cores(): return lax.ppermute(a, 'prow', [(i, i ^ 1) for i in range(32)])  7.03 us
    ppermute x2, starting transfers between devices, z_fill(): below = lax.ppermute(second, 'pcol', [(i, (i - 1) % 8) for i in range(8)])  6.35 us
    ppermute x9, waiting for transfers between devices, gather_ring(): got[d] = lax.ppermute(piece, 'prow', pairs)  5.77 us
    ppermute x2, starting transfers between devices, z_out(): down = lax.ppermute(b, 'pcol', [(0, 6), (1, 7), (2, 0)])  4.68 us
  transfers between devices with their start and end apart: 20, of which 7 were waited for; matrix products, arithmetic and copies ran while one was open for 0% of the time, Pallas kernels for 4%

commit v1 on v0

--- a/solution.py
+++ b/solution.py
@@ -33,9 +33,9 @@
         return self.flags[other]
 
 
-def gather_ring(piece, x_core):
+def gather_ring(piece, x_core, order=(2, 1, 3)):
     got = {}
-    for d in (2, 1, 3):
+    for d in order:
         pairs = []
         for y in range(4):
             for x in range(4):
@@ -86,9 +86,9 @@
                 for r in range(3):
                     at = 192 * j + 48 * i + 16 * r
                     part = bulk[at : at + 16, :]
-                    abuf[r, rows, 128 * half : 128 * half + 128] = part[:, 0:128]
-                    lane = 256 + 896 * half
-                    abuf[r, rows, lane : lane + 896] = part[:, 128:1024]
+                    for k in range(8):
+                        lane = 256 * k + 128 * half
+                        abuf[r, rows, lane : lane + 128] = part[:, 128 * k : 128 * k + 128]
                     for q in range(2):
                         at = 384 * j + 128 * r + 64 * q + 16 * i
                         cbuf[r, q, rows, 128 * half : 128 * half + 128] = corner[at : at + 16, :]
@@ -197,13 +197,8 @@
     w = matrix.reshape(256, 2048)
     panel = w[:, :256]
     up, down = z_out(panel, z)
-    halves = jnp.stack(
-        [
-            jnp.concatenate([w[:, :128], w[:, 256:1152]], axis=1),
-            jnp.concatenate([w[:, 128:256], w[:, 1152:]], axis=1),
-        ]
-    )
-    parts = halves.reshape(2, 16, 16, 1024).transpose(1, 0, 2, 3).reshape(32, 16, 1024)
+    parts = matrix.reshape(16, 16, 8, 2, 128).transpose(0, 3, 1, 2, 4)
+    parts = parts.reshape(32, 16, 8, 128)
     piece = lax.all_to_all(parts, "prow", 0, 0)[:3].reshape(48, 1024)
     piece, up, down = tie(piece, up, down)
     line = jnp.concatenate(gather_ring(piece, 0))
@@ -218,7 +213,7 @@
         ]
     )
     edge_out = z_out(edge, z)
-    mine = gather_ring(line, 1)
+    mine = gather_ring(line, 1, (1, 3, 2))
     *mine, edge_up, edge_down = tie(*mine, *edge_out)
     mine = jnp.concatenate(mine)
     other = swap_cores(mine)

time: 79.6 us -> 79 us (level)
  other arithmetic: 1.51 us -> 0.3 us
  local copies, waits for them, and re-layouts: 1.86 us -> 3 us
    transpose x0 -> x1, local copies, waits for them, and re-layouts: none -> 2.44 us  [body(): parts = matrix.reshape(16, 16, 8, 2, 128).transpose(0, 3, 1, 2, 4)]
    unnamed x13 -> x16, local copies, waits for them, and re-layouts: 1.67 us -> 0.47 us
    another operation x1 -> x0, other arithmetic: 1.07 us -> none  [body(): jnp.stack([jnp.concatenate([w[:, :128], w[:, 256:1152]], axis=1), jnp.con...]
  transfers between devices with their start and end apart: 20 -> 20, of which waited for: 7 -> 8; matrix products, arithmetic and copies ran while one was open for 0% -> 1% of each run, Pallas kernels for 4% -> 4%
where the time goes in v1:
time: 79 us; the launch traced here: 78.7 us
  starting transfers between devices  49.4 us (63%)
  waiting for transfers between devices  18.3 us (23%)
  Pallas kernels  7.35 us (9%)
  local copies, waits for them, and re-layouts  3 us (4%)
    ppermute x2, starting transfers between devices, z_out(): up = lax.ppermute(b, 'pcol', [(0, 3), (1, 4), (2, 5)])  12.6 us
    ppermute x9, starting transfers between devices, gather_ring(): got[d] = lax.ppermute(piece, 'prow', pairs)  10.5 us
    all_to_all x1, starting transfers between devices, body(): piece = lax.all_to_all(parts, 'prow', 0, 0)[:3].reshape(48, 1024)  8.72 us
    all_to_all x1, waiting for transfers between devices, body(): piece = lax.all_to_all(parts, 'prow', 0, 0)[:3].reshape(48, 1024)  8.22 us
    ppermute x2, starting transfers between devices, swap_cores(): return lax.ppermute(a, 'prow', [(i, i ^ 1) for i in range(32)])  6.73 us
    ppermute x2, starting transfers between devices, z_fill(): below = lax.ppermute(second, 'pcol', [(i, (i - 1) % 8) for i in range(8)])  6.05 us
    ppermute x9, waiting for transfers between devices, gather_ring(): got[d] = lax.ppermute(piece, 'prow', pairs)  5.98 us
    ppermute x2, starting transfers between devices, z_out(): down = lax.ppermute(b, 'pcol', [(0, 6), (1, 7), (2, 0)])  4.68 us
  transfers between devices with their start and end apart: 20, of which 8 were waited for; matrix products, arithmetic and copies ran while one was open for 1% of the time, Pallas kernels for 4%

profile of v1, /device:TPU:1, one launch (start us, length us, event | category | flops | bytes accessed | tf_op | source)
XLA Modules:
  0.0 78.7 jit_solution(12333002361966605007)
XLA Ops:
  0.0 0.1 pad_add_fusion.s_ref
  0.1 2.4 %copy.4 = bf16[16,2,16,8,128]{4,3,2,1,0:T(8,128)(2,1)} copy(bf16[16,2,16,8,128]{4,3,1,2,0:T(8,128)(2,1)} %bitcast.19) | data formatting | bytes 2097152 | tf_op jit(solution)/shard_map/transpose | solution.py:200
  2.5 8.7 %all-to-all-start = ((bf16[32,16,8,128]{3,2,1,0:T(8,128)(2,1)}), bf16[32,16,8,128]{3,2,1,0:T(8,128)(2,1)S(1)}, u32[]{:S(2)}, u32[]{:S(2)}) async-start(bf16[32,16,8,128]{3,2,1,0:T(8,128)(2,1)} %bitcast.4), calls=%async_computation | async-start | bytes 2097152 | tf_op jit(solution)/shard_map/all_to_all | solution.py:202
  11.3 0.3 copy.7
  11.6 6.3 %collective-permute-start = (bf16[256,256]{1,0:T(8,128)(2,1)S(1)}, bf16[256,256]{1,0:T(8,128)(2,1)S(1)}, u32[]{:S(2)}, u32[]{:S(2)}) collective-permute-start(bf16[256,256]{1,0:T(8,128)(2,1)S(1)} %slice.57), channel_id=1, source_target_pairs={{0,3},{1,4},{2,5},{8,11},{9,12},{10,13},{16,19},{17,20},{18,21},{2... | collective-permute-start | bytes 393224 | tf_op jit(solution)/shard_map/ppermute | solution.py:53
  17.9 2.3 %collective-permute-start.1 = (bf16[256,256]{1,0:T(8,128)(2,1)S(1)}, bf16[256,256]{1,0:T(8,128)(2,1)S(1)}, u32[]{:S(2)}, u32[]{:S(2)}) collective-permute-start(bf16[256,256]{1,0:T(8,128)(2,1)S(1)} %slice.57), channel_id=1, source_target_pairs={{0,6},{1,7},{2,0},{8,14},{9,15},{10,8},{16,22},{17,23},{18,16},{24... | collective-permute-start | bytes 393224 | tf_op jit(solution)/shard_map/ppermute | solution.py:54
  20.2 8.2 %all-to-all-done = bf16[32,16,8,128]{3,2,1,0:T(8,128)(2,1)S(1)} async-done(((bf16[32,16,8,128]{3,2,1,0:T(8,128)(2,1)}), bf16[32,16,8,128]{3,2,1,0:T(8,128)(2,1)S(1)}, u32[]{:S(2)}, u32[]{:S(2)}) %all-to-all-start) | async-done | bytes 1048608 | tf_op jit(solution)/shard_map/all_to_all | solution.py:202
  28.5 0.1 collective-permute-start.2
  28.6 1.7 %collective-permute-start.3 = (bf16[48,1024]{1,0:T(8,128)(2,1)S(1)}, bf16[48,1024]{1,0:T(8,128)(2,1)S(1)}, u32[]{:S(2)}, u32[]{:S(2)}) collective-permute-start(bf16[48,1024]{1,0:T(8,128)(2,1)S(1)} %bitcast.22), channel_id=1, source_target_pairs={{0,32},{8,136},{16,48},{24,152},{32,0},{40,168},{48,16},{56,184},{... | collective-permute-start | bytes 294920 | tf_op jit(solution)/shard_map/ppermute | solution.py:44
  30.3 1.4 %collective-permute-start.4 = (bf16[48,1024]{1,0:T(8,128)(2,1)S(1)}, bf16[48,1024]{1,0:T(8,128)(2,1)S(1)}, u32[]{:S(2)}, u32[]{:S(2)}) collective-permute-start(bf16[48,1024]{1,0:T(8,128)(2,1)S(1)} %bitcast.23), channel_id=1, source_target_pairs={{0,48},{8,200},{16,0},{24,216},{32,16},{40,232},{48,32},{56,248},{... | collective-permute-start | bytes 294920 | tf_op jit(solution)/shard_map/ppermute | solution.py:44
  31.7 2.9 %collective-permute-done.2 = bf16[48,1024]{1,0:T(8,128)(2,1)S(1)} collective-permute-done((bf16[48,1024]{1,0:T(8,128)(2,1)S(1)}, bf16[48,1024]{1,0:T(8,128)(2,1)S(1)}, u32[]{:S(2)}, u32[]{:S(2)}) %collective-permute-start.2) | collective-permute-done | bytes 98336 | tf_op jit(solution)/shard_map/ppermute | solution.py:44
  34.6 0.5 collective-permute-done.4
  35.2 0.4 collective-permute-start.5
  35.6 1.8 %collective-permute-start.6 = (bf16[192,1024]{1,0:T(8,128)(2,1)S(1)}, bf16[192,1024]{1,0:T(8,128)(2,1)S(1)}, u32[]{:S(2)}, u32[]{:S(2)}) collective-permute-start(bf16[192,1024]{1,0:T(8,128)(2,1)S(1)} %constant_dynamic-update-slice_fusion), channel_id=1, source_target_pairs={{8,40},{0,128},{24,56},{16,144},{40,8},{32,160},{56,24},{48,176},{... | collective-permute-start | bytes 1179656 | tf_op jit(solution)/shard_map/ppermute | solution.py:44
  37.4 0.8 %collective-permute-start.7 = (bf16[192,1024]{1,0:T(8,128)(2,1)S(1)}, bf16[192,1024]{1,0:T(8,128)(2,1)S(1)}, u32[]{:S(2)}, u32[]{:S(2)}) collective-permute-start(bf16[192,1024]{1,0:T(8,128)(2,1)S(1)} %constant_dynamic-update-slice_fusion), channel_id=1, source_target_pairs={{8,56},{0,192},{24,8},{16,208},{40,24},{32,224},{56,40},{48,240},{... | collective-permute-start | bytes 1179656 | tf_op jit(solution)/shard_map/ppermute | solution.py:44
  38.3 6.3 %collective-permute-start.8 = (bf16[128,128]{1,0:T(8,128)(2,1)S(1)}, bf16[128,128]{1,0:T(8,128)(2,1)S(1)}, u32[]{:S(2)}, u32[]{:S(2)}) collective-permute-start(bf16[128,128]{1,0:T(8,128)(2,1)S(1)} %pad_maximum_fusion.1), channel_id=1, source_target_pairs={{0,3},{1,4},{2,5},{8,11},{9,12},{10,13},{16,19},{17,20},{18,21},{2... | collective-permute-start | bytes 98312 | tf_op jit(solution)/shard_map/ppermute | solution.py:53
  44.6 2.3 %collective-permute-start.9 = (bf16[128,128]{1,0:T(8,128)(2,1)S(1)}, bf16[128,128]{1,0:T(8,128)(2,1)S(1)}, u32[]{:S(2)}, u32[]{:S(2)}) collective-permute-start(bf16[128,128]{1,0:T(8,128)(2,1)S(1)} %pad_maximum_fusion.1), channel_id=1, source_target_pairs={{0,6},{1,7},{2,0},{8,14},{9,15},{10,8},{16,22},{17,23},{18,16},{24... | collective-permute-start | bytes 98312 | tf_op jit(solution)/shard_map/ppermute | solution.py:54
  47.0 4.0 %collective-permute-done.9 = bf16[128,128]{1,0:T(8,128)(2,1)S(1)} collective-permute-done((bf16[128,128]{1,0:T(8,128)(2,1)S(1)}, bf16[128,128]{1,0:T(8,128)(2,1)S(1)}, u32[]{:S(2)}, u32[]{:S(2)}) %collective-permute-start.9) | collective-permute-done | bytes 32800 | tf_op jit(solution)/shard_map/ppermute | solution.py:54
  51.1 0.1 collective-permute-start.11
  51.2 2.8 %collective-permute-start.12 = (bf16[128,128]{1,0:T(8,128)(2,1)S(1)}, bf16[128,128]{1,0:T(8,128)(2,1)S(1)}, u32[]{:S(2)}, u32[]{:S(2)}) collective-permute-start(bf16[128,128]{1,0:T(8,128)(2,1)S(1)} %get-tuple-element.61), channel_id=1, source_target_pairs={{0,7},{1,0},{2,1},{3,2},{4,3},{5,4},{6,5},{7,6},{8,15},{9,8},{10,9... | collective-permute-start | bytes 98312 | tf_op jit(solution)/shard_map/ppermute | solution.py:62
  54.2 4.5 %collective-permute-start.10 = (bf16[768,1024]{1,0:T(8,128)(2,1)S(1)}, bf16[768,1024]{1,0:T(8,128)(2,1)S(1)}, u32[]{:S(2)}, u32[]{:S(2)}) collective-permute-start(bf16[768,1024]{1,0:T(8,128)(2,1)S(1)} %constant_dynamic-update-slice_fusion.4.mine), channel_id=1, source_target_pairs={{0,8},{8,0},{16,24},{24,16},{32,40},{40,32},{48,56},{56,48},{64,72... | collective-permute-start | bytes 4718600 | tf_op jit(solution)/shard_map/ppermute | solution.py:189
  58.8 1.6 %collective-permute-start.14 = (bf16[384,128]{1,0:T(8,128)(2,1)S(1)}, bf16[384,128]{1,0:T(8,128)(2,1)S(1)}, u32[]{:S(2)}, u32[]{:S(2)}) collective-permute-start(bf16[384,128]{1,0:T(8,128)(2,1)S(1)} %pad_maximum_fusion), channel_id=1, source_target_pairs={{8,40},{0,128},{24,56},{16,144},{40,8},{32,160},{56,24},{48,176},{... | collective-permute-start | bytes 294920 | tf_op jit(solution)/shard_map/ppermute | solution.py:44
  60.4 1.5 %collective-permute-start.13 = (bf16[384,128]{1,0:T(8,128)(2,1)S(1)}, bf16[384,128]{1,0:T(8,128)(2,1)S(1)}, u32[]{:S(2)}, u32[]{:S(2)}) collective-permute-start(bf16[384,128]{1,0:T(8,128)(2,1)S(1)} %pad_maximum_fusion), channel_id=1, source_target_pairs={{8,24},{0,64},{24,40},{16,80},{40,56},{32,96},{56,8},{48,112},{72,... | collective-permute-start | bytes 294920 | tf_op jit(solution)/shard_map/ppermute | solution.py:44
  61.9 1.2 %collective-permute-start.15 = (bf16[384,128]{1,0:T(8,128)(2,1)S(1)}, bf16[384,128]{1,0:T(8,128)(2,1)S(1)}, u32[]{:S(2)}, u32[]{:S(2)}) collective-permute-start(bf16[384,128]{1,0:T(8,128)(2,1)S(1)} %pad_maximum_fusion), channel_id=1, source_target_pairs={{8,56},{0,192},{24,8},{16,208},{40,24},{32,224},{56,40},{48,240},{... | collective-permute-start | bytes 294920 | tf_op jit(solution)/shard_map/ppermute | solution.py:44
  63.1 0.8 collective-permute-done.14
  63.9 1.5 %collective-permute-done.13 = bf16[384,128]{1,0:T(8,128)(2,1)S(1)} collective-permute-done((bf16[384,128]{1,0:T(8,128)(2,1)S(1)}, bf16[384,128]{1,0:T(8,128)(2,1)S(1)}, u32[]{:S(2)}, u32[]{:S(2)}) %collective-permute-start.13) | collective-permute-done | bytes 98336 | tf_op jit(solution)/shard_map/ppermute | solution.py:44
  65.4 0.2 collective-permute-done.15
  65.7 2.2 %collective-permute-start.16 = (bf16[1536,128]{1,0:T(8,128)(2,1)S(1)}, bf16[1536,128]{1,0:T(8,128)(2,1)S(1)}, u32[]{:S(2)}, u32[]{:S(2)}) collective-permute-start(bf16[1536,128]{1,0:T(8,128)(2,1)S(1)} %constant_dynamic-update-slice_fusion.8.cmine), channel_id=1, source_target_pairs={{0,8},{8,0},{16,24},{24,16},{32,40},{40,32},{48,56},{56,48},{64,72... | collective-permute-start | bytes 1179656 | tf_op jit(solution)/shard_map/ppermute | solution.py:189
  67.9 0.1 collective-permute-start.17
  68.0 3.2 %collective-permute-start.18 = (bf16[256,256]{1,0:T(8,128)(2,1)S(1)}, bf16[256,256]{1,0:T(8,128)(2,1)S(1)}, u32[]{:S(2)}, u32[]{:S(2)}) collective-permute-start(bf16[256,256]{1,0:T(8,128)(2,1)S(1)} %get-tuple-element.53.own5), channel_id=1, source_target_pairs={{0,7},{1,0},{2,1},{3,2},{4,3},{5,4},{6,5},{7,6},{8,15},{9,8},{10,9... | collective-permute-start | bytes 393224 | tf_op jit(solution)/shard_map/ppermute | solution.py:62
  71.3 3.5 %shard_map.37 = (bf16[768,2048]{1,0:T(8,128)(2,1)S(1)}, bf16[3,256,256]{2,1,0:T(8,128)(2,1)S(1)}, f32[256,256]{1,0:T(8,128)S(1)}) custom-call(s32[2]{0:T(128)S(1)} %pad_add_fusion.s_ref, bf16[768,1024]{1,0:T(8,128)(2,1)S(1)} %constant_dynamic-update-slice_fusion.4.mine, bf16[768,1024]{1,0:T(8,128)(2,1)S(1)} %collective-permute-done.10.other, ...), custom_call_target="tpu_custom_call" | custom-call | flops 1700000000 | bytes 10000000 | tf_op jit(solution)/shard_map/pallas_call | solution.py:127
  74.8 3.9 %shard_map.38 = f32[4096,128]{1,0:T(8,128)} custom-call(s32[2]{0:T(128)S(1)} %pad_add_fusion.s_ref, bf16[768,2048]{1,0:T(8,128)(2,1)S(1)} %get-tuple-element.48.u, bf16[3,256,256]{2,1,0:T(8,128)(2,1)S(1)} %get-tuple-element.49.small, f32[256,256]{1,0:T(8,128)S(1)} %get-tuple-element.50.diag, bf16[256,2048]{1,0:T(8,128)(2,1)S(1)} %bitcast.18, ...), custom_call_target="tpu_custom_call" | custom-call | flops 900000000 | bytes 7000000 | tf_op jit(solution)/shard_map/pallas_call | solution.py:174
  (45 shorter events, 0.6 us)
Async XLA Ops:
  2.5 8.7 %copy-start.2 = (bf16[1,1,256,8,1,256]{5,3,4,2,1,0:T(8,128)(2,1)S(1)}, bf16[1,1,256,8,1,256]{5,3,4,2,1,0:T(8,128)(2,1)}, u32[]{:S(2)}) copy-start(bf16[1,1,256,8,1,256]{5,3,4,2,1,0:T(8,128)(2,1)} %param.3) | copy-start | bytes 3145732
  2.5 25.9 %all-to-all-start = ((bf16[32,16,8,128]{3,2,1,0:T(8,128)(2,1)}), bf16[32,16,8,128]{3,2,1,0:T(8,128)(2,1)S(1)}, u32[]{:S(2)}, u32[]{:S(2)}) async-start(bf16[32,16,8,128]{3,2,1,0:T(8,128)(2,1)} %bitcast.4), calls=%async_computation | async-start | bytes 2097152 | tf_op jit(solution)/shard_map/all_to_all | solution.py:202
  11.6 16.9 %collective-permute-start = (bf16[256,256]{1,0:T(8,128)(2,1)S(1)}, bf16[256,256]{1,0:T(8,128)(2,1)S(1)}, u32[]{:S(2)}, u32[]{:S(2)}) collective-permute-start(bf16[256,256]{1,0:T(8,128)(2,1)S(1)} %slice.57), channel_id=1, source_target_pairs={{0,3},{1,4},{2,5},{8,11},{9,12},{10,13},{16,19},{17,20},{18,21},{2... | collective-permute-start | bytes 393224 | tf_op jit(solution)/shard_map/ppermute | solution.py:53
  17.9 10.6 %collective-permute-start.1 = (bf16[256,256]{1,0:T(8,128)(2,1)S(1)}, bf16[256,256]{1,0:T(8,128)(2,1)S(1)}, u32[]{:S(2)}, u32[]{:S(2)}) collective-permute-start(bf16[256,256]{1,0:T(8,128)(2,1)S(1)} %slice.57), channel_id=1, source_target_pairs={{0,6},{1,7},{2,0},{8,14},{9,15},{10,8},{16,22},{17,23},{18,16},{24... | collective-permute-start | bytes 393224 | tf_op jit(solution)/shard_map/ppermute | solution.py:54
  28.5 6.1 %collective-permute-start.2 = (bf16[48,1024]{1,0:T(8,128)(2,1)S(1)}, bf16[48,1024]{1,0:T(8,128)(2,1)S(1)}, u32[]{:S(2)}, u32[]{:S(2)}) collective-permute-start(bf16[48,1024]{1,0:T(8,128)(2,1)S(1)} %bitcast.21), channel_id=1, source_target_pairs={{0,16},{8,72},{16,32},{24,88},{32,48},{40,104},{48,0},{56,120},{64... | collective-permute-start | bytes 294920 | tf_op jit(solution)/shard_map/ppermute | solution.py:44
  28.6 6.0 %collective-permute-start.3 = (bf16[48,1024]{1,0:T(8,128)(2,1)S(1)}, bf16[48,1024]{1,0:T(8,128)(2,1)S(1)}, u32[]{:S(2)}, u32[]{:S(2)}) collective-permute-start(bf16[48,1024]{1,0:T(8,128)(2,1)S(1)} %bitcast.22), channel_id=1, source_target_pairs={{0,32},{8,136},{16,48},{24,152},{32,0},{40,168},{48,16},{56,184},{... | collective-permute-start | bytes 294920 | tf_op jit(solution)/shard_map/ppermute | solution.py:44
  30.3 4.9 %collective-permute-start.4 = (bf16[48,1024]{1,0:T(8,128)(2,1)S(1)}, bf16[48,1024]{1,0:T(8,128)(2,1)S(1)}, u32[]{:S(2)}, u32[]{:S(2)}) collective-permute-start(bf16[48,1024]{1,0:T(8,128)(2,1)S(1)} %bitcast.23), channel_id=1, source_target_pairs={{0,48},{8,200},{16,0},{24,216},{32,16},{40,232},{48,32},{56,248},{... | collective-permute-start | bytes 294920 | tf_op jit(solution)/shard_map/ppermute | solution.py:44
  35.2 15.8 %collective-permute-start.5 = (bf16[192,1024]{1,0:T(8,128)(2,1)S(1)}, bf16[192,1024]{1,0:T(8,128)(2,1)S(1)}, u32[]{:S(2)}, u32[]{:S(2)}) collective-permute-start(bf16[192,1024]{1,0:T(8,128)(2,1)S(1)} %constant_dynamic-update-slice_fusion), channel_id=1, source_target_pairs={{8,24},{0,64},{24,40},{16,80},{40,56},{32,96},{56,8},{48,112},{72,... | collective-permute-start | bytes 1179656 | tf_op jit(solution)/shard_map/ppermute | solution.py:44
  35.6 15.4 %collective-permute-start.6 = (bf16[192,1024]{1,0:T(8,128)(2,1)S(1)}, bf16[192,1024]{1,0:T(8,128)(2,1)S(1)}, u32[]{:S(2)}, u32[]{:S(2)}) collective-permute-start(bf16[192,1024]{1,0:T(8,128)(2,1)S(1)} %constant_dynamic-update-slice_fusion), channel_id=1, source_target_pairs={{8,40},{0,128},{24,56},{16,144},{40,8},{32,160},{56,24},{48,176},{... | collective-permute-start | bytes 1179656 | tf_op jit(solution)/shard_map/ppermute | solution.py:44
  37.4 13.6 %collective-permute-start.7 = (bf16[192,1024]{1,0:T(8,128)(2,1)S(1)}, bf16[192,1024]{1,0:T(8,128)(2,1)S(1)}, u32[]{:S(2)}, u32[]{:S(2)}) collective-permute-start(bf16[192,1024]{1,0:T(8,128)(2,1)S(1)} %constant_dynamic-update-slice_fusion), channel_id=1, source_target_pairs={{8,56},{0,192},{24,8},{16,208},{40,24},{32,224},{56,40},{48,240},{... | collective-permute-start | bytes 1179656 | tf_op jit(solution)/shard_map/ppermute | solution.py:44
  38.3 8.7 %collective-permute-start.8 = (bf16[128,128]{1,0:T(8,128)(2,1)S(1)}, bf16[128,128]{1,0:T(8,128)(2,1)S(1)}, u32[]{:S(2)}, u32[]{:S(2)}) collective-permute-start(bf16[128,128]{1,0:T(8,128)(2,1)S(1)} %pad_maximum_fusion.1), channel_id=1, source_target_pairs={{0,3},{1,4},{2,5},{8,11},{9,12},{10,13},{16,19},{17,20},{18,21},{2... | collective-permute-start | bytes 98312 | tf_op jit(solution)/shard_map/ppermute | solution.py:53
  44.6 6.4 %collective-permute-start.9 = (bf16[128,128]{1,0:T(8,128)(2,1)S(1)}, bf16[128,128]{1,0:T(8,128)(2,1)S(1)}, u32[]{:S(2)}, u32[]{:S(2)}) collective-permute-start(bf16[128,128]{1,0:T(8,128)(2,1)S(1)} %pad_maximum_fusion.1), channel_id=1, source_target_pairs={{0,6},{1,7},{2,0},{8,14},{9,15},{10,8},{16,22},{17,23},{18,16},{24... | collective-permute-start | bytes 98312 | tf_op jit(solution)/shard_map/ppermute | solution.py:54
  51.1 7.6 %collective-permute-start.11 = (bf16[128,128]{1,0:T(8,128)(2,1)S(1)}, bf16[128,128]{1,0:T(8,128)(2,1)S(1)}, u32[]{:S(2)}, u32[]{:S(2)}) collective-permute-start(bf16[128,128]{1,0:T(8,128)(2,1)S(1)} %get-tuple-element.62), channel_id=1, source_target_pairs={{0,1},{1,2},{2,3},{3,4},{4,5},{5,6},{6,7},{7,0},{8,9},{9,10},{10,1... | collective-permute-start | bytes 98312 | tf_op jit(solution)/shard_map/ppermute | solution.py:61
  51.2 7.5 %collective-permute-start.12 = (bf16[128,128]{1,0:T(8,128)(2,1)S(1)}, bf16[128,128]{1,0:T(8,128)(2,1)S(1)}, u32[]{:S(2)}, u32[]{:S(2)}) collective-permute-start(bf16[128,128]{1,0:T(8,128)(2,1)S(1)} %get-tuple-element.61), channel_id=1, source_target_pairs={{0,7},{1,0},{2,1},{3,2},{4,3},{5,4},{6,5},{7,6},{8,15},{9,8},{10,9... | collective-permute-start | bytes 98312 | tf_op jit(solution)/shard_map/ppermute | solution.py:62
  54.1 17.2 %copy-start = (bf16[3,256,256]{2,1,0:T(8,128)(2,1)S(1)}, bf16[3,256,256]{2,1,0:T(8,128)(2,1)}, u32[]{:S(2)}) copy-start(bf16[3,256,256]{2,1,0:T(8,128)(2,1)} %uinv.3) | copy-start | bytes 1179652
  54.1 17.1 %copy-start.1 = (bf16[3,256,256]{2,1,0:T(8,128)(2,1)S(1)}, bf16[3,256,256]{2,1,0:T(8,128)(2,1)}, u32[]{:S(2)}) copy-start(bf16[3,256,256]{2,1,0:T(8,128)(2,1)} %linv.1) | copy-start | bytes 1179652
  54.2 17.1 %collective-permute-start.10 = (bf16[768,1024]{1,0:T(8,128)(2,1)S(1)}, bf16[768,1024]{1,0:T(8,128)(2,1)S(1)}, u32[]{:S(2)}, u32[]{:S(2)}) collective-permute-start(bf16[768,1024]{1,0:T(8,128)(2,1)S(1)} %constant_dynamic-update-slice_fusion.4.mine), channel_id=1, source_target_pairs={{0,8},{8,0},{16,24},{24,16},{32,40},{40,32},{48,56},{56,48},{64,72... | collective-permute-start | bytes 4718600 | tf_op jit(solution)/shard_map/ppermute | solution.py:189
  58.8 5.1 %collective-permute-start.14 = (bf16[384,128]{1,0:T(8,128)(2,1)S(1)}, bf16[384,128]{1,0:T(8,128)(2,1)S(1)}, u32[]{:S(2)}, u32[]{:S(2)}) collective-permute-start(bf16[384,128]{1,0:T(8,128)(2,1)S(1)} %pad_maximum_fusion), channel_id=1, source_target_pairs={{8,40},{0,128},{24,56},{16,144},{40,8},{32,160},{56,24},{48,176},{... | collective-permute-start | bytes 294920 | tf_op jit(solution)/shard_map/ppermute | solution.py:44
  60.4 5.0 %collective-permute-start.13 = (bf16[384,128]{1,0:T(8,128)(2,1)S(1)}, bf16[384,128]{1,0:T(8,128)(2,1)S(1)}, u32[]{:S(2)}, u32[]{:S(2)}) collective-permute-start(bf16[384,128]{1,0:T(8,128)(2,1)S(1)} %pad_maximum_fusion), channel_id=1, source_target_pairs={{8,24},{0,64},{24,40},{16,80},{40,56},{32,96},{56,8},{48,112},{72,... | collective-permute-start | bytes 294920 | tf_op jit(solution)/shard_map/ppermute | solution.py:44
  61.9 3.8 %collective-permute-start.15 = (bf16[384,128]{1,0:T(8,128)(2,1)S(1)}, bf16[384,128]{1,0:T(8,128)(2,1)S(1)}, u32[]{:S(2)}, u32[]{:S(2)}) collective-permute-start(bf16[384,128]{1,0:T(8,128)(2,1)S(1)} %pad_maximum_fusion), channel_id=1, source_target_pairs={{8,56},{0,192},{24,8},{16,208},{40,24},{32,224},{56,40},{48,240},{... | collective-permute-start | bytes 294920 | tf_op jit(solution)/shard_map/ppermute | solution.py:44
  65.7 5.6 %collective-permute-start.16 = (bf16[1536,128]{1,0:T(8,128)(2,1)S(1)}, bf16[1536,128]{1,0:T(8,128)(2,1)S(1)}, u32[]{:S(2)}, u32[]{:S(2)}) collective-permute-start(bf16[1536,128]{1,0:T(8,128)(2,1)S(1)} %constant_dynamic-update-slice_fusion.8.cmine), channel_id=1, source_target_pairs={{0,8},{8,0},{16,24},{24,16},{32,40},{40,32},{48,56},{56,48},{64,72... | collective-permute-start | bytes 1179656 | tf_op jit(solution)/shard_map/ppermute | solution.py:189
  67.9 6.9 %collective-permute-start.17 = (bf16[256,256]{1,0:T(8,128)(2,1)S(1)}, bf16[256,256]{1,0:T(8,128)(2,1)S(1)}, u32[]{:S(2)}, u32[]{:S(2)}) collective-permute-start(bf16[256,256]{1,0:T(8,128)(2,1)S(1)} %get-tuple-element.54.own), channel_id=1, source_target_pairs={{0,1},{1,2},{2,3},{3,4},{4,5},{5,6},{6,7},{7,0},{8,9},{9,10},{10,1... | collective-permute-start | bytes 393224 | tf_op jit(solution)/shard_map/ppermute | solution.py:61
  68.0 6.8 %collective-permute-start.18 = (bf16[256,256]{1,0:T(8,128)(2,1)S(1)}, bf16[256,256]{1,0:T(8,128)(2,1)S(1)}, u32[]{:S(2)}, u32[]{:S(2)}) collective-permute-start(bf16[256,256]{1,0:T(8,128)(2,1)S(1)} %get-tuple-element.53.own5), channel_id=1, source_target_pairs={{0,7},{1,0},{2,1},{3,2},{4,3},{5,4},{6,5},{7,6},{8,15},{9,8},{10,9... | collective-permute-start | bytes 393224 | tf_op jit(solution)/shard_map/ppermute | solution.py:62

commit v2 on v1

--- a/solution.py
+++ b/solution.py
@@ -33,7 +33,7 @@
         return self.flags[other]
 
 
-def gather_ring(piece, x_core, order=(2, 1, 3)):
+def gather_ring(piece, x_core, order=(1, 3, 2)):
     got = {}
     for d in order:
         pairs = []
@@ -213,7 +213,7 @@
         ]
     )
     edge_out = z_out(edge, z)
-    mine = gather_ring(line, 1, (1, 3, 2))
+    mine = gather_ring(line, 1)
     *mine, edge_up, edge_down = tie(*mine, *edge_out)
     mine = jnp.concatenate(mine)
     other = swap_cores(mine)

time: 79 us -> 79 us (level)
  no operation moved by 1% of the time
where the time goes in v2:
time: 79 us; the launch traced here: 78.7 us
  starting transfers between devices  49.4 us (63%)
  waiting for transfers between devices  18.3 us (23%)
  Pallas kernels  7.35 us (9%)
  local copies, waits for them, and re-layouts  3 us (4%)
    ppermute x2, starting transfers between devices, z_out(): up = lax.ppermute(b, 'pcol', [(0, 3), (1, 4), (2, 5)])  12.6 us
    ppermute x9, starting transfers between devices, gather_ring(): got[d] = lax.ppermute(piece, 'prow', pairs)  10.5 us
    all_to_all x1, starting transfers between devices, body(): piece = lax.all_to_all(parts, 'prow', 0, 0)[:3].reshape(48, 1024)  8.72 us
    all_to_all x1, waiting for transfers between devices, body(): piece = lax.all_to_all(parts, 'prow', 0, 0)[:3].reshape(48, 1024)  8.22 us
    ppermute x2, starting transfers between devices, swap_cores(): return lax.ppermute(a, 'prow', [(i, i ^ 1) for i in range(32)])  6.73 us
    ppermute x2, starting transfers between devices, z_fill(): below = lax.ppermute(second, 'pcol', [(i, (i - 1) % 8) for i in range(8)])  6.05 us
    ppermute x9, waiting for transfers between devices, gather_ring(): got[d] = lax.ppermute(piece, 'prow', pairs)  5.98 us
    ppermute x2, starting transfers between devices, z_out(): down = lax.ppermute(b, 'pcol', [(0, 6), (1, 7), (2, 0)])  4.68 us
  transfers between devices with their start and end apart: 20, of which 8 were waited for; matrix products, arithmetic and copies ran while one was open for 1% of the time, Pallas kernels for 4%

profile of v2, /device:TPU:1, one launch (start us, length us, event | category | flops | bytes accessed | tf_op | source)
XLA Modules:
  0.0 78.7 jit_solution(12333002361966605007)
XLA Ops:
  0.0 0.1 pad_add_fusion.s_ref
  0.1 2.4 %copy.4 = bf16[16,2,16,8,128]{4,3,2,1,0:T(8,128)(2,1)} copy(bf16[16,2,16,8,128]{4,3,1,2,0:T(8,128)(2,1)} %bitcast.19) | data formatting | bytes 2097152 | tf_op jit(solution)/shard_map/transpose | solution.py:200
  2.5 8.7 %all-to-all-start = ((bf16[32,16,8,128]{3,2,1,0:T(8,128)(2,1)}), bf16[32,16,8,128]{3,2,1,0:T(8,128)(2,1)S(1)}, u32[]{:S(2)}, u32[]{:S(2)}) async-start(bf16[32,16,8,128]{3,2,1,0:T(8,128)(2,1)} %bitcast.4), calls=%async_computation | async-start | bytes 2097152 | tf_op jit(solution)/shard_map/all_to_all | solution.py:202
  11.3 0.3 copy.7
  11.6 6.3 %collective-permute-start = (bf16[256,256]{1,0:T(8,128)(2,1)S(1)}, bf16[256,256]{1,0:T(8,128)(2,1)S(1)}, u32[]{:S(2)}, u32[]{:S(2)}) collective-permute-start(bf16[256,256]{1,0:T(8,128)(2,1)S(1)} %slice.57), channel_id=1, source_target_pairs={{0,3},{1,4},{2,5},{8,11},{9,12},{10,13},{16,19},{17,20},{18,21},{2... | collective-permute-start | bytes 393224 | tf_op jit(solution)/shard_map/ppermute | solution.py:53
  17.9 2.3 %collective-permute-start.1 = (bf16[256,256]{1,0:T(8,128)(2,1)S(1)}, bf16[256,256]{1,0:T(8,128)(2,1)S(1)}, u32[]{:S(2)}, u32[]{:S(2)}) collective-permute-start(bf16[256,256]{1,0:T(8,128)(2,1)S(1)} %slice.57), channel_id=1, source_target_pairs={{0,6},{1,7},{2,0},{8,14},{9,15},{10,8},{16,22},{17,23},{18,16},{24... | collective-permute-start | bytes 393224 | tf_op jit(solution)/shard_map/ppermute | solution.py:54
  20.2 8.2 %all-to-all-done = bf16[32,16,8,128]{3,2,1,0:T(8,128)(2,1)S(1)} async-done(((bf16[32,16,8,128]{3,2,1,0:T(8,128)(2,1)}), bf16[32,16,8,128]{3,2,1,0:T(8,128)(2,1)S(1)}, u32[]{:S(2)}, u32[]{:S(2)}) %all-to-all-start) | async-done | bytes 1048608 | tf_op jit(solution)/shard_map/all_to_all | solution.py:202
  28.5 0.1 collective-permute-start.2
  28.6 1.7 %collective-permute-start.3 = (bf16[48,1024]{1,0:T(8,128)(2,1)S(1)}, bf16[48,1024]{1,0:T(8,128)(2,1)S(1)}, u32[]{:S(2)}, u32[]{:S(2)}) collective-permute-start(bf16[48,1024]{1,0:T(8,128)(2,1)S(1)} %bitcast.22), channel_id=1, source_target_pairs={{0,32},{8,136},{16,48},{24,152},{32,0},{40,168},{48,16},{56,184},{... | collective-permute-start | bytes 294920 | tf_op jit(solution)/shard_map/ppermute | solution.py:44
  30.3 1.4 %collective-permute-start.4 = (bf16[48,1024]{1,0:T(8,128)(2,1)S(1)}, bf16[48,1024]{1,0:T(8,128)(2,1)S(1)}, u32[]{:S(2)}, u32[]{:S(2)}) collective-permute-start(bf16[48,1024]{1,0:T(8,128)(2,1)S(1)} %bitcast.23), channel_id=1, source_target_pairs={{0,48},{8,200},{16,0},{24,216},{32,16},{40,232},{48,32},{56,248},{... | collective-permute-start | bytes 294920 | tf_op jit(solution)/shard_map/ppermute | solution.py:44
  31.7 2.9 %collective-permute-done.2 = bf16[48,1024]{1,0:T(8,128)(2,1)S(1)} collective-permute-done((bf16[48,1024]{1,0:T(8,128)(2,1)S(1)}, bf16[48,1024]{1,0:T(8,128)(2,1)S(1)}, u32[]{:S(2)}, u32[]{:S(2)}) %collective-permute-start.2) | collective-permute-done | bytes 98336 | tf_op jit(solution)/shard_map/ppermute | solution.py:44
  34.6 0.5 collective-permute-done.4
  35.2 0.4 collective-permute-start.5
  35.6 1.8 %collective-permute-start.6 = (bf16[192,1024]{1,0:T(8,128)(2,1)S(1)}, bf16[192,1024]{1,0:T(8,128)(2,1)S(1)}, u32[]{:S(2)}, u32[]{:S(2)}) collective-permute-start(bf16[192,1024]{1,0:T(8,128)(2,1)S(1)} %constant_dynamic-update-slice_fusion), channel_id=1, source_target_pairs={{8,40},{0,128},{24,56},{16,144},{40,8},{32,160},{56,24},{48,176},{... | collective-permute-start | bytes 1179656 | tf_op jit(solution)/shard_map/ppermute | solution.py:44
  37.4 0.8 %collective-permute-start.7 = (bf16[192,1024]{1,0:T(8,128)(2,1)S(1)}, bf16[192,1024]{1,0:T(8,128)(2,1)S(1)}, u32[]{:S(2)}, u32[]{:S(2)}) collective-permute-start(bf16[192,1024]{1,0:T(8,128)(2,1)S(1)} %constant_dynamic-update-slice_fusion), channel_id=1, source_target_pairs={{8,56},{0,192},{24,8},{16,208},{40,24},{32,224},{56,40},{48,240},{... | collective-permute-start | bytes 1179656 | tf_op jit(solution)/shard_map/ppermute | solution.py:44
  38.3 6.3 %collective-permute-start.8 = (bf16[128,128]{1,0:T(8,128)(2,1)S(1)}, bf16[128,128]{1,0:T(8,128)(2,1)S(1)}, u32[]{:S(2)}, u32[]{:S(2)}) collective-permute-start(bf16[128,128]{1,0:T(8,128)(2,1)S(1)} %pad_maximum_fusion.1), channel_id=1, source_target_pairs={{0,3},{1,4},{2,5},{8,11},{9,12},{10,13},{16,19},{17,20},{18,21},{2... | collective-permute-start | bytes 98312 | tf_op jit(solution)/shard_map/ppermute | solution.py:53
  44.6 2.3 %collective-permute-start.9 = (bf16[128,128]{1,0:T(8,128)(2,1)S(1)}, bf16[128,128]{1,0:T(8,128)(2,1)S(1)}, u32[]{:S(2)}, u32[]{:S(2)}) collective-permute-start(bf16[128,128]{1,0:T(8,128)(2,1)S(1)} %pad_maximum_fusion.1), channel_id=1, source_target_pairs={{0,6},{1,7},{2,0},{8,14},{9,15},{10,8},{16,22},{17,23},{18,16},{24... | collective-permute-start | bytes 98312 | tf_op jit(solution)/shard_map/ppermute | solution.py:54
  47.0 4.0 %collective-permute-done.9 = bf16[128,128]{1,0:T(8,128)(2,1)S(1)} collective-permute-done((bf16[128,128]{1,0:T(8,128)(2,1)S(1)}, bf16[128,128]{1,0:T(8,128)(2,1)S(1)}, u32[]{:S(2)}, u32[]{:S(2)}) %collective-permute-start.9) | collective-permute-done | bytes 32800 | tf_op jit(solution)/shard_map/ppermute | solution.py:54
  51.1 0.1 collective-permute-start.11
  51.2 2.8 %collective-permute-start.12 = (bf16[128,128]{1,0:T(8,128)(2,1)S(1)}, bf16[128,128]{1,0:T(8,128)(2,1)S(1)}, u32[]{:S(2)}, u32[]{:S(2)}) collective-permute-start(bf16[128,128]{1,0:T(8,128)(2,1)S(1)} %get-tuple-element.61), channel_id=1, source_target_pairs={{0,7},{1,0},{2,1},{3,2},{4,3},{5,4},{6,5},{7,6},{8,15},{9,8},{10,9... | collective-permute-start | bytes 98312 | tf_op jit(solution)/shard_map/ppermute | solution.py:62
  54.2 4.5 %collective-permute-start.10 = (bf16[768,1024]{1,0:T(8,128)(2,1)S(1)}, bf16[768,1024]{1,0:T(8,128)(2,1)S(1)}, u32[]{:S(2)}, u32[]{:S(2)}) collective-permute-start(bf16[768,1024]{1,0:T(8,128)(2,1)S(1)} %constant_dynamic-update-slice_fusion.4.mine), channel_id=1, source_target_pairs={{0,8},{8,0},{16,24},{24,16},{32,40},{40,32},{48,56},{56,48},{64,72... | collective-permute-start | bytes 4718600 | tf_op jit(solution)/shard_map/ppermute | solution.py:189
  58.8 1.6 %collective-permute-start.14 = (bf16[384,128]{1,0:T(8,128)(2,1)S(1)}, bf16[384,128]{1,0:T(8,128)(2,1)S(1)}, u32[]{:S(2)}, u32[]{:S(2)}) collective-permute-start(bf16[384,128]{1,0:T(8,128)(2,1)S(1)} %pad_maximum_fusion), channel_id=1, source_target_pairs={{8,40},{0,128},{24,56},{16,144},{40,8},{32,160},{56,24},{48,176},{... | collective-permute-start | bytes 294920 | tf_op jit(solution)/shard_map/ppermute | solution.py:44
  60.4 1.5 %collective-permute-start.13 = (bf16[384,128]{1,0:T(8,128)(2,1)S(1)}, bf16[384,128]{1,0:T(8,128)(2,1)S(1)}, u32[]{:S(2)}, u32[]{:S(2)}) collective-permute-start(bf16[384,128]{1,0:T(8,128)(2,1)S(1)} %pad_maximum_fusion), channel_id=1, source_target_pairs={{8,24},{0,64},{24,40},{16,80},{40,56},{32,96},{56,8},{48,112},{72,... | collective-permute-start | bytes 294920 | tf_op jit(solution)/shard_map/ppermute | solution.py:44
  61.9 1.2 %collective-permute-start.15 = (bf16[384,128]{1,0:T(8,128)(2,1)S(1)}, bf16[384,128]{1,0:T(8,128)(2,1)S(1)}, u32[]{:S(2)}, u32[]{:S(2)}) collective-permute-start(bf16[384,128]{1,0:T(8,128)(2,1)S(1)} %pad_maximum_fusion), channel_id=1, source_target_pairs={{8,56},{0,192},{24,8},{16,208},{40,24},{32,224},{56,40},{48,240},{... | collective-permute-start | bytes 294920 | tf_op jit(solution)/shard_map/ppermute | solution.py:44
  63.1 0.8 collective-permute-done.14
  63.9 1.5 %collective-permute-done.13 = bf16[384,128]{1,0:T(8,128)(2,1)S(1)} collective-permute-done((bf16[384,128]{1,0:T(8,128)(2,1)S(1)}, bf16[384,128]{1,0:T(8,128)(2,1)S(1)}, u32[]{:S(2)}, u32[]{:S(2)}) %collective-permute-start.13) | collective-permute-done | bytes 98336 | tf_op jit(solution)/shard_map/ppermute | solution.py:44
  65.4 0.2 collective-permute-done.15
  65.7 2.2 %collective-permute-start.16 = (bf16[1536,128]{1,0:T(8,128)(2,1)S(1)}, bf16[1536,128]{1,0:T(8,128)(2,1)S(1)}, u32[]{:S(2)}, u32[]{:S(2)}) collective-permute-start(bf16[1536,128]{1,0:T(8,128)(2,1)S(1)} %constant_dynamic-update-slice_fusion.8.cmine), channel_id=1, source_target_pairs={{0,8},{8,0},{16,24},{24,16},{32,40},{40,32},{48,56},{56,48},{64,72... | collective-permute-start | bytes 1179656 | tf_op jit(solution)/shard_map/ppermute | solution.py:189
  67.9 0.1 collective-permute-start.17
  68.0 3.2 %collective-permute-start.18 = (bf16[256,256]{1,0:T(8,128)(2,1)S(1)}, bf16[256,256]{1,0:T(8,128)(2,1)S(1)}, u32[]{:S(2)}, u32[]{:S(2)}) collective-permute-start(bf16[256,256]{1,0:T(8,128)(2,1)S(1)} %get-tuple-element.53.own5), channel_id=1, source_target_pairs={{0,7},{1,0},{2,1},{3,2},{4,3},{5,4},{6,5},{7,6},{8,15},{9,8},{10,9... | collective-permute-start | bytes 393224 | tf_op jit(solution)/shard_map/ppermute | solution.py:62
  71.3 3.5 %shard_map.37 = (bf16[768,2048]{1,0:T(8,128)(2,1)S(1)}, bf16[3,256,256]{2,1,0:T(8,128)(2,1)S(1)}, f32[256,256]{1,0:T(8,128)S(1)}) custom-call(s32[2]{0:T(128)S(1)} %pad_add_fusion.s_ref, bf16[768,1024]{1,0:T(8,128)(2,1)S(1)} %constant_dynamic-update-slice_fusion.4.mine, bf16[768,1024]{1,0:T(8,128)(2,1)S(1)} %collective-permute-done.10.other, ...), custom_call_target="tpu_custom_call" | custom-call | flops 1700000000 | bytes 10000000 | tf_op jit(solution)/shard_map/pallas_call | solution.py:127
  74.8 3.9 %shard_map.38 = f32[4096,128]{1,0:T(8,128)} custom-call(s32[2]{0:T(128)S(1)} %pad_add_fusion.s_ref, bf16[768,2048]{1,0:T(8,128)(2,1)S(1)} %get-tuple-element.48.u, bf16[3,256,256]{2,1,0:T(8,128)(2,1)S(1)} %get-tuple-element.49.small, f32[256,256]{1,0:T(8,128)S(1)} %get-tuple-element.50.diag, bf16[256,2048]{1,0:T(8,128)(2,1)S(1)} %bitcast.18, ...), custom_call_target="tpu_custom_call" | custom-call | flops 900000000 | bytes 7000000 | tf_op jit(solution)/shard_map/pallas_call | solution.py:174
  (45 shorter events, 0.6 us)
Async XLA Ops:
  2.5 8.7 %copy-start.2 = (bf16[1,1,256,8,1,256]{5,3,4,2,1,0:T(8,128)(2,1)S(1)}, bf16[1,1,256,8,1,256]{5,3,4,2,1,0:T(8,128)(2,1)}, u32[]{:S(2)}) copy-start(bf16[1,1,256,8,1,256]{5,3,4,2,1,0:T(8,128)(2,1)} %param.3) | copy-start | bytes 3145732
  2.5 25.9 %all-to-all-start = ((bf16[32,16,8,128]{3,2,1,0:T(8,128)(2,1)}), bf16[32,16,8,128]{3,2,1,0:T(8,128)(2,1)S(1)}, u32[]{:S(2)}, u32[]{:S(2)}) async-start(bf16[32,16,8,128]{3,2,1,0:T(8,128)(2,1)} %bitcast.4), calls=%async_computation | async-start | bytes 2097152 | tf_op jit(solution)/shard_map/all_to_all | solution.py:202
  11.6 16.9 %collective-permute-start = (bf16[256,256]{1,0:T(8,128)(2,1)S(1)}, bf16[256,256]{1,0:T(8,128)(2,1)S(1)}, u32[]{:S(2)}, u32[]{:S(2)}) collective-permute-start(bf16[256,256]{1,0:T(8,128)(2,1)S(1)} %slice.57), channel_id=1, source_target_pairs={{0,3},{1,4},{2,5},{8,11},{9,12},{10,13},{16,19},{17,20},{18,21},{2... | collective-permute-start | bytes 393224 | tf_op jit(solution)/shard_map/ppermute | solution.py:53
  17.9 10.6 %collective-permute-start.1 = (bf16[256,256]{1,0:T(8,128)(2,1)S(1)}, bf16[256,256]{1,0:T(8,128)(2,1)S(1)}, u32[]{:S(2)}, u32[]{:S(2)}) collective-permute-start(bf16[256,256]{1,0:T(8,128)(2,1)S(1)} %slice.57), channel_id=1, source_target_pairs={{0,6},{1,7},{2,0},{8,14},{9,15},{10,8},{16,22},{17,23},{18,16},{24... | collective-permute-start | bytes 393224 | tf_op jit(solution)/shard_map/ppermute | solution.py:54
  28.5 6.1 %collective-permute-start.2 = (bf16[48,1024]{1,0:T(8,128)(2,1)S(1)}, bf16[48,1024]{1,0:T(8,128)(2,1)S(1)}, u32[]{:S(2)}, u32[]{:S(2)}) collective-permute-start(bf16[48,1024]{1,0:T(8,128)(2,1)S(1)} %bitcast.21), channel_id=1, source_target_pairs={{0,16},{8,72},{16,32},{24,88},{32,48},{40,104},{48,0},{56,120},{64... | collective-permute-start | bytes 294920 | tf_op jit(solution)/shard_map/ppermute | solution.py:44
  28.6 6.0 %collective-permute-start.3 = (bf16[48,1024]{1,0:T(8,128)(2,1)S(1)}, bf16[48,1024]{1,0:T(8,128)(2,1)S(1)}, u32[]{:S(2)}, u32[]{:S(2)}) collective-permute-start(bf16[48,1024]{1,0:T(8,128)(2,1)S(1)} %bitcast.22), channel_id=1, source_target_pairs={{0,32},{8,136},{16,48},{24,152},{32,0},{40,168},{48,16},{56,184},{... | collective-permute-start | bytes 294920 | tf_op jit(solution)/shard_map/ppermute | solution.py:44
  30.3 4.9 %collective-permute-start.4 = (bf16[48,1024]{1,0:T(8,128)(2,1)S(1)}, bf16[48,1024]{1,0:T(8,128)(2,1)S(1)}, u32[]{:S(2)}, u32[]{:S(2)}) collective-permute-start(bf16[48,1024]{1,0:T(8,128)(2,1)S(1)} %bitcast.23), channel_id=1, source_target_pairs={{0,48},{8,200},{16,0},{24,216},{32,16},{40,232},{48,32},{56,248},{... | collective-permute-start | bytes 294920 | tf_op jit(solution)/shard_map/ppermute | solution.py:44
  35.2 15.8 %collective-permute-start.5 = (bf16[192,1024]{1,0:T(8,128)(2,1)S(1)}, bf16[192,1024]{1,0:T(8,128)(2,1)S(1)}, u32[]{:S(2)}, u32[]{:S(2)}) collective-permute-start(bf16[192,1024]{1,0:T(8,128)(2,1)S(1)} %constant_dynamic-update-slice_fusion), channel_id=1, source_target_pairs={{8,24},{0,64},{24,40},{16,80},{40,56},{32,96},{56,8},{48,112},{72,... | collective-permute-start | bytes 1179656 | tf_op jit(solution)/shard_map/ppermute | solution.py:44
  35.6 15.4 %collective-permute-start.6 = (bf16[192,1024]{1,0:T(8,128)(2,1)S(1)}, bf16[192,1024]{1,0:T(8,128)(2,1)S(1)}, u32[]{:S(2)}, u32[]{:S(2)}) collective-permute-start(bf16[192,1024]{1,0:T(8,128)(2,1)S(1)} %constant_dynamic-update-slice_fusion), channel_id=1, source_target_pairs={{8,40},{0,128},{24,56},{16,144},{40,8},{32,160},{56,24},{48,176},{... | collective-permute-start | bytes 1179656 | tf_op jit(solution)/shard_map/ppermute | solution.py:44
  37.4 13.6 %collective-permute-start.7 = (bf16[192,1024]{1,0:T(8,128)(2,1)S(1)}, bf16[192,1024]{1,0:T(8,128)(2,1)S(1)}, u32[]{:S(2)}, u32[]{:S(2)}) collective-permute-start(bf16[192,1024]{1,0:T(8,128)(2,1)S(1)} %constant_dynamic-update-slice_fusion), channel_id=1, source_target_pairs={{8,56},{0,192},{24,8},{16,208},{40,24},{32,224},{56,40},{48,240},{... | collective-permute-start | bytes 1179656 | tf_op jit(solution)/shard_map/ppermute | solution.py:44
  38.3 8.7 %collective-permute-start.8 = (bf16[128,128]{1,0:T(8,128)(2,1)S(1)}, bf16[128,128]{1,0:T(8,128)(2,1)S(1)}, u32[]{:S(2)}, u32[]{:S(2)}) collective-permute-start(bf16[128,128]{1,0:T(8,128)(2,1)S(1)} %pad_maximum_fusion.1), channel_id=1, source_target_pairs={{0,3},{1,4},{2,5},{8,11},{9,12},{10,13},{16,19},{17,20},{18,21},{2... | collective-permute-start | bytes 98312 | tf_op jit(solution)/shard_map/ppermute | solution.py:53
  44.6 6.4 %collective-permute-start.9 = (bf16[128,128]{1,0:T(8,128)(2,1)S(1)}, bf16[128,128]{1,0:T(8,128)(2,1)S(1)}, u32[]{:S(2)}, u32[]{:S(2)}) collective-permute-start(bf16[128,128]{1,0:T(8,128)(2,1)S(1)} %pad_maximum_fusion.1), channel_id=1, source_target_pairs={{0,6},{1,7},{2,0},{8,14},{9,15},{10,8},{16,22},{17,23},{18,16},{24... | collective-permute-start | bytes 98312 | tf_op jit(solution)/shard_map/ppermute | solution.py:54
  51.1 7.6 %collective-permute-start.11 = (bf16[128,128]{1,0:T(8,128)(2,1)S(1)}, bf16[128,128]{1,0:T(8,128)(2,1)S(1)}, u32[]{:S(2)}, u32[]{:S(2)}) collective-permute-start(bf16[128,128]{1,0:T(8,128)(2,1)S(1)} %get-tuple-element.62), channel_id=1, source_target_pairs={{0,1},{1,2},{2,3},{3,4},{4,5},{5,6},{6,7},{7,0},{8,9},{9,10},{10,1... | collective-permute-start | bytes 98312 | tf_op jit(solution)/shard_map/ppermute | solution.py:61
  51.2 7.5 %collective-permute-start.12 = (bf16[128,128]{1,0:T(8,128)(2,1)S(1)}, bf16[128,128]{1,0:T(8,128)(2,1)S(1)}, u32[]{:S(2)}, u32[]{:S(2)}) collective-permute-start(bf16[128,128]{1,0:T(8,128)(2,1)S(1)} %get-tuple-element.61), channel_id=1, source_target_pairs={{0,7},{1,0},{2,1},{3,2},{4,3},{5,4},{6,5},{7,6},{8,15},{9,8},{10,9... | collective-permute-start | bytes 98312 | tf_op jit(solution)/shard_map/ppermute | solution.py:62
  54.1 17.2 %copy-start = (bf16[3,256,256]{2,1,0:T(8,128)(2,1)S(1)}, bf16[3,256,256]{2,1,0:T(8,128)(2,1)}, u32[]{:S(2)}) copy-start(bf16[3,256,256]{2,1,0:T(8,128)(2,1)} %uinv.3) | copy-start | bytes 1179652
  54.1 17.1 %copy-start.1 = (bf16[3,256,256]{2,1,0:T(8,128)(2,1)S(1)}, bf16[3,256,256]{2,1,0:T(8,128)(2,1)}, u32[]{:S(2)}) copy-start(bf16[3,256,256]{2,1,0:T(8,128)(2,1)} %linv.1) | copy-start | bytes 1179652
  54.2 17.1 %collective-permute-start.10 = (bf16[768,1024]{1,0:T(8,128)(2,1)S(1)}, bf16[768,1024]{1,0:T(8,128)(2,1)S(1)}, u32[]{:S(2)}, u32[]{:S(2)}) collective-permute-start(bf16[768,1024]{1,0:T(8,128)(2,1)S(1)} %constant_dynamic-update-slice_fusion.4.mine), channel_id=1, source_target_pairs={{0,8},{8,0},{16,24},{24,16},{32,40},{40,32},{48,56},{56,48},{64,72... | collective-permute-start | bytes 4718600 | tf_op jit(solution)/shard_map/ppermute | solution.py:189
  58.8 5.1 %collective-permute-start.14 = (bf16[384,128]{1,0:T(8,128)(2,1)S(1)}, bf16[384,128]{1,0:T(8,128)(2,1)S(1)}, u32[]{:S(2)}, u32[]{:S(2)}) collective-permute-start(bf16[384,128]{1,0:T(8,128)(2,1)S(1)} %pad_maximum_fusion), channel_id=1, source_target_pairs={{8,40},{0,128},{24,56},{16,144},{40,8},{32,160},{56,24},{48,176},{... | collective-permute-start | bytes 294920 | tf_op jit(solution)/shard_map/ppermute | solution.py:44
  60.4 5.0 %collective-permute-start.13 = (bf16[384,128]{1,0:T(8,128)(2,1)S(1)}, bf16[384,128]{1,0:T(8,128)(2,1)S(1)}, u32[]{:S(2)}, u32[]{:S(2)}) collective-permute-start(bf16[384,128]{1,0:T(8,128)(2,1)S(1)} %pad_maximum_fusion), channel_id=1, source_target_pairs={{8,24},{0,64},{24,40},{16,80},{40,56},{32,96},{56,8},{48,112},{72,... | collective-permute-start | bytes 294920 | tf_op jit(solution)/shard_map/ppermute | solution.py:44
  61.9 3.8 %collective-permute-start.15 = (bf16[384,128]{1,0:T(8,128)(2,1)S(1)}, bf16[384,128]{1,0:T(8,128)(2,1)S(1)}, u32[]{:S(2)}, u32[]{:S(2)}) collective-permute-start(bf16[384,128]{1,0:T(8,128)(2,1)S(1)} %pad_maximum_fusion), channel_id=1, source_target_pairs={{8,56},{0,192},{24,8},{16,208},{40,24},{32,224},{56,40},{48,240},{... | collective-permute-start | bytes 294920 | tf_op jit(solution)/shard_map/ppermute | solution.py:44
  65.7 5.6 %collective-permute-start.16 = (bf16[1536,128]{1,0:T(8,128)(2,1)S(1)}, bf16[1536,128]{1,0:T(8,128)(2,1)S(1)}, u32[]{:S(2)}, u32[]{:S(2)}) collective-permute-start(bf16[1536,128]{1,0:T(8,128)(2,1)S(1)} %constant_dynamic-update-slice_fusion.8.cmine), channel_id=1, source_target_pairs={{0,8},{8,0},{16,24},{24,16},{32,40},{40,32},{48,56},{56,48},{64,72... | collective-permute-start | bytes 1179656 | tf_op jit(solution)/shard_map/ppermute | solution.py:189
  67.9 6.9 %collective-permute-start.17 = (bf16[256,256]{1,0:T(8,128)(2,1)S(1)}, bf16[256,256]{1,0:T(8,128)(2,1)S(1)}, u32[]{:S(2)}, u32[]{:S(2)}) collective-permute-start(bf16[256,256]{1,0:T(8,128)(2,1)S(1)} %get-tuple-element.54.own), channel_id=1, source_target_pairs={{0,1},{1,2},{2,3},{3,4},{4,5},{5,6},{6,7},{7,0},{8,9},{9,10},{10,1... | collective-permute-start | bytes 393224 | tf_op jit(solution)/shard_map/ppermute | solution.py:61
  68.0 6.8 %collective-permute-start.18 = (bf16[256,256]{1,0:T(8,128)(2,1)S(1)}, bf16[256,256]{1,0:T(8,128)(2,1)S(1)}, u32[]{:S(2)}, u32[]{:S(2)}) collective-permute-start(bf16[256,256]{1,0:T(8,128)(2,1)S(1)} %get-tuple-element.53.own5), channel_id=1, source_target_pairs={{0,7},{1,0},{2,1},{3,2},{4,3},{5,4},{6,5},{7,6},{8,15},{9,8},{10,9... | collective-permute-start | bytes 393224 | tf_op jit(solution)/shard_map/ppermute | solution.py:62
